TPU v7x, 32 devices: a whole 2x2x4 slice. The times are simulated.
32 devices in a mesh: dp: 16 (over z, x, core), tensor: 2 (over y).
Axes of the slice: x: 2, y: 2, z: 4, core: 2. Of those that a mesh axis runs over, the one named last changes fastest.
Arguments:
- tokens: bfloat16 [16, 1024, 1152], P('dp', 'tensor'), may hold values from -6 to 6
- segments: int32 [16, 1024], P('dp'), may hold values from 0 to 3, as said below
- labels: int32 [16, 4], P('dp'), may hold values from 0 to 1000
- timesteps: int32 [16, 4], P('dp'), may hold values from 0 to 999
- class_table: float32 [1001, 1152], replicated, may hold values from -6 to 6
- time_weight: float32 [256, 1152], replicated, may hold values from -0.5 to 0.5
- ada_weight: bfloat16 [1152, 6912], P(None, 'tensor'), may hold values from -0.1875 to 0.1875
- qkv_weight: bfloat16 [1152, 3, 1152], P(None, None, 'tensor'), may hold values from -0.1875 to 0.1875
- proj_weight: bfloat16 [1152, 1152], P('tensor'), may hold values from -0.75 to 0.75
- up_weight: bfloat16 [1152, 4608], P(None, 'tensor'), may hold values from -0.1875 to 0.1875
- down_weight: bfloat16 [4608, 1152], P('tensor'), may hold values from -0.09375 to 0.09375
- cotangent: bfloat16 [16, 1024, 1152], P('dp', 'tensor'), may hold values from -6 to 6
Outputs:
- output: bfloat16 [16, 1024, 1152], P('dp', 'tensor')
- grad_tokens: bfloat16 [16, 1024, 1152], P('dp', 'tensor')
- grad_class_table: float32 [1001, 1152], replicated
- grad_time_weight: float32 [256, 1152], replicated
- grad_ada_weight: float32 [1152, 6912], P(None, 'tensor')
- grad_qkv_weight: float32 [1152, 3, 1152], P(None, None, 'tensor')
- grad_proj_weight: float32 [1152, 1152], P('tensor')
- grad_up_weight: float32 [1152, 4608], P(None, 'tensor')
- grad_down_weight: float32 [4608, 1152], P('tensor')
Inputs may be any that keep to these rules, and one draw needn't show every extreme that they name: `segments`: slots of a pack are numbered from 0 by the samples present; each sample has 1024 or 256 tokens, the same number on each of the pack's blocks of 512 positions, where its tokens are consecutive and ids never fall within a block; the samples fill the pack; some pack holds only samples of 256 tokens and some only samples of 1024.
All inputs are finite; a program needn't handle non-finite values.
Results may differ from a plain program's by a relative error of at most 0.025.
The roundings to bfloat16 on the way count: a program that leaves them out, or rounds other values in their place, can miss the bound.
Values may be sent and summed in bfloat16 or wider, within the bound.
No kernel may reach another device: no remote copies, remote signals or barrier semaphores. Data moves between devices by JAX's collectives and lax.ppermute only.
A program may use at most 256 MiB of HBM per device.

v0:
```python
import math

import jax
import jax.numpy as jnp
from jax import lax
from jax.sharding import PartitionSpec as P

HEAD_DIM = 72


HIGH = lax.Precision.HIGHEST


def features(steps_f, width_total):
    half = width_total // 2
    freqs = jnp.exp(-math.log(10000.0) * jnp.arange(half, dtype=jnp.float32) / half)
    angles = steps_f[:, None] * freqs[None, :]
    return jnp.concatenate([jnp.cos(angles), jnp.sin(angles)], axis=1)


def normalize(values):
    average = jnp.mean(values, axis=-1, keepdims=True)
    centred = values - average
    inverse = lax.rsqrt(jnp.mean(centred * centred, axis=-1, keepdims=True) + 1e-06)
    return (centred * inverse, inverse)


def norm_back(grad_normed, normed, inverse):
    first = jnp.mean(grad_normed, axis=-1, keepdims=True)
    second = jnp.mean(grad_normed * normed, axis=-1, keepdims=True)
    return inverse * (grad_normed - first - normed * second)


def contract_rows(left, right):
    return lax.dot_general(
        left, right, (((0,), (0,)), ((), ())), preferred_element_type=jnp.float32
    )


def contract_exact(left, right):
    return lax.dot_general(
        left, right, (((0,), (0,)), ((), ())), precision=HIGH, preferred_element_type=jnp.float32
    )


def times_transposed(left, right):
    return lax.dot_general(
        left, right, (((1,), (1,)), ((), ())), preferred_element_type=jnp.float32
    )


def body(
    tokens,
    segments,
    labels,
    timesteps,
    class_table,
    time_weight,
    ada_weight,
    qkv_weight,
    proj_weight,
    up_weight,
    down_weight,
    cotangent,
):
    own_tokens = tokens[0].astype(jnp.float32)
    shard_rows = own_tokens.shape[0]
    model_width = own_tokens.shape[1]
    seg_all = segments[0]
    pack_rows = seg_all.shape[0]
    slot_count = labels.shape[1]
    class_count = class_table.shape[0]
    freq_width = time_weight.shape[0]
    local_width = qkv_weight.shape[2]
    head_count = local_width // HEAD_DIM
    scale_factor = 1.0 / math.sqrt(HEAD_DIM)
    position = lax.axis_index("tensor")
    seg_own = lax.dynamic_slice_in_dim(seg_all, position * shard_rows, shard_rows)
    own_hot = (seg_own[:, None] == jnp.arange(slot_count, dtype=jnp.int32)[None, :]).astype(
        jnp.float32
    )
    label_hot = (labels[0][:, None] == jnp.arange(class_count, dtype=jnp.int32)[None, :]).astype(
        jnp.float32
    )
    step_feats = features(timesteps[0].astype(jnp.float32), freq_width)
    condition = jnp.dot(label_hot, class_table, precision=HIGH) + jnp.dot(
        step_feats, time_weight, precision=HIGH
    )
    act_low = jax.nn.silu(condition).astype(jnp.bfloat16)
    mod_part = jnp.dot(act_low, ada_weight, preferred_element_type=jnp.float32)
    modulation = lax.all_gather(mod_part, "tensor", axis=1, tiled=True)
    per_token = jnp.dot(own_hot, modulation, precision=HIGH)
    shift_one, scale_one, gate_one, shift_two, scale_two, gate_two = jnp.split(per_token, 6, axis=1)
    normed_one, inverse_one = normalize(own_tokens)
    modulated_one = (normed_one * (1.0 + scale_one) + shift_one).astype(jnp.bfloat16)
    inputs_one = lax.all_gather(modulated_one, "tensor", axis=0, tiled=True)
    qkv_flat = qkv_weight.reshape(model_width, 3 * local_width)
    qkv = jnp.dot(inputs_one, qkv_flat, preferred_element_type=jnp.float32).astype(jnp.bfloat16)
    qkv_heads = qkv.reshape(pack_rows, 3, head_count, HEAD_DIM).transpose(1, 2, 0, 3)
    queries = qkv_heads[0]
    keys = qkv_heads[1]
    values = qkv_heads[2]
    block = min(512, pack_rows)
    block_count = pack_rows // block
    starts = jnp.arange(block_count, dtype=jnp.int32) * block

    def scores_of(start):
        query_block = lax.dynamic_slice_in_dim(queries, start, block, 1)
        seg_block = lax.dynamic_slice_in_dim(seg_all, start, block)
        raw = (
            jnp.einsum("hqd,hkd->hqk", query_block, keys, preferred_element_type=jnp.float32)
            * scale_factor
        )
        same = (seg_block[:, None] == seg_all[None, :])[None]
        return (jnp.where(same, raw, -1e30), query_block)

    def attend(start):
        scores = scores_of(start)[0]
        top = jnp.max(scores, axis=-1, keepdims=True)
        exps = jnp.exp(scores - top)
        total = jnp.sum(exps, axis=-1, keepdims=True)
        weights = (exps / total).astype(jnp.bfloat16)
        out_block = jnp.einsum("hqk,hkd->hqd", weights, values, preferred_element_type=jnp.float32)
        return (out_block, (top + jnp.log(total))[..., 0])

    out_blocks, lse_blocks = lax.map(attend, starts)
    attended = out_blocks.transpose(0, 2, 1, 3).reshape(pack_rows, local_width).astype(jnp.bfloat16)
    lse_all = lse_blocks.transpose(1, 0, 2).reshape(head_count, pack_rows)
    branch_one = lax.psum_scatter(
        jnp.dot(attended, proj_weight, preferred_element_type=jnp.float32),
        "tensor",
        scatter_dimension=0,
        tiled=True,
    )
    halfway = own_tokens + gate_one * branch_one
    normed_two, inverse_two = normalize(halfway)
    modulated_two = (normed_two * (1.0 + scale_two) + shift_two).astype(jnp.bfloat16)
    inputs_two = lax.all_gather(modulated_two, "tensor", axis=0, tiled=True)
    hidden = jnp.dot(inputs_two, up_weight, preferred_element_type=jnp.float32)
    active = jax.nn.gelu(hidden, approximate=True).astype(jnp.bfloat16)
    branch_two = lax.psum_scatter(
        jnp.dot(active, down_weight, preferred_element_type=jnp.float32).astype(jnp.bfloat16),
        "tensor",
        scatter_dimension=0,
        tiled=True,
    ).astype(jnp.float32)
    result = halfway + gate_two * branch_two
    grad_out = cotangent[0].astype(jnp.float32)
    grad_gate_two = grad_out * branch_two
    grad_branch_two = (grad_out * gate_two).astype(jnp.bfloat16)
    grads_two = lax.all_gather(grad_branch_two, "tensor", axis=0, tiled=True)
    grad_down = contract_rows(active, grads_two)
    grad_active = times_transposed(grads_two, down_weight)
    gelu_back = jax.vjp(lambda inner: jax.nn.gelu(inner, approximate=True), hidden)[1]
    grad_hidden = gelu_back(grad_active)[0].astype(jnp.bfloat16)
    grad_up = contract_rows(inputs_two, grad_hidden)
    grad_mod_two = lax.psum_scatter(
        times_transposed(grad_hidden, up_weight), "tensor", scatter_dimension=0, tiled=True
    )
    grad_halfway = grad_out + norm_back(grad_mod_two * (1.0 + scale_two), normed_two, inverse_two)
    grad_gate_one = grad_halfway * branch_one
    grad_branch_one = (grad_halfway * gate_one).astype(jnp.bfloat16)
    grads_one = lax.all_gather(grad_branch_one, "tensor", axis=0, tiled=True)
    grad_proj = contract_rows(attended, grads_one)
    grad_attended = times_transposed(grads_one, proj_weight).astype(jnp.bfloat16)
    grad_heads = grad_attended.reshape(pack_rows, head_count, HEAD_DIM).transpose(1, 0, 2)

    def attend_back(carry, start):
        grad_keys, grad_values = carry
        scores, query_block = scores_of(start)
        lse_block = lax.dynamic_slice_in_dim(lse_all, start, block, 1)
        probs = jnp.exp(scores - lse_block[..., None])
        grad_block = lax.dynamic_slice_in_dim(grad_heads, start, block, 1)
        grad_probs = jnp.einsum(
            "hqd,hkd->hqk", grad_block, values, preferred_element_type=jnp.float32
        )
        grad_scores = (
            probs * (grad_probs - jnp.sum(probs * grad_probs, axis=-1, keepdims=True))
        ).astype(jnp.bfloat16)
        grad_query = (
            jnp.einsum("hqk,hkd->hqd", grad_scores, keys, preferred_element_type=jnp.float32)
            * scale_factor
        )
        grad_keys = (
            grad_keys
            + jnp.einsum(
                "hqk,hqd->hkd", grad_scores, query_block, preferred_element_type=jnp.float32
            )
            * scale_factor
        )
        grad_values = grad_values + jnp.einsum(
            "hqk,hqd->hkd",
            probs.astype(jnp.bfloat16),
            grad_block,
            preferred_element_type=jnp.float32,
        )
        return ((grad_keys, grad_values), grad_query)

    empty = jnp.zeros((head_count, pack_rows, HEAD_DIM), jnp.float32)
    key_grads, grad_queries = lax.scan(attend_back, (empty, empty), starts)
    query_grads = grad_queries.transpose(1, 0, 2, 3).reshape(head_count, pack_rows, HEAD_DIM)
    grad_stack = jnp.stack([query_grads, key_grads[0], key_grads[1]], axis=0)
    grad_qkv = (
        grad_stack.transpose(2, 0, 1, 3).reshape(pack_rows, 3 * local_width).astype(jnp.bfloat16)
    )
    grad_qkv_weight = contract_rows(inputs_one, grad_qkv).reshape(model_width, 3, local_width)
    grad_mod_one = lax.psum_scatter(
        times_transposed(grad_qkv, qkv_flat).astype(jnp.bfloat16),
        "tensor",
        scatter_dimension=0,
        tiled=True,
    ).astype(jnp.float32)
    grad_input = grad_halfway + norm_back(grad_mod_one * (1.0 + scale_one), normed_one, inverse_one)
    grad_per_token = jnp.concatenate(
        [
            grad_mod_one,
            grad_mod_one * normed_one,
            grad_gate_one,
            grad_mod_two,
            grad_mod_two * normed_two,
            grad_gate_two,
        ],
        axis=1,
    )
    slot_terms = contract_exact(own_hot, grad_per_token)
    grad_modulation = lax.psum_scatter(
        slot_terms.astype(jnp.bfloat16), "tensor", scatter_dimension=1, tiled=True
    )
    grad_ada = contract_rows(act_low, grad_modulation)
    cond_part = times_transposed(grad_modulation, ada_weight)
    grad_activated = lax.psum(cond_part.astype(jnp.bfloat16), "tensor").astype(jnp.float32)
    grad_condition = jax.vjp(jax.nn.silu, condition)[1](grad_activated)[0]
    grad_class = contract_exact(label_hot, grad_condition)
    grad_time = contract_exact(step_feats, grad_condition)
    summed = (
        lax.psum(grad_class.astype(jnp.bfloat16), "dp").astype(jnp.float32),
        lax.psum(grad_time.astype(jnp.bfloat16), "dp").astype(jnp.float32),
        lax.psum(grad_ada.astype(jnp.bfloat16), "dp").astype(jnp.float32),
        lax.psum(grad_qkv_weight.astype(jnp.bfloat16), "dp").astype(jnp.float32),
        lax.psum(grad_proj.astype(jnp.bfloat16), "dp").astype(jnp.float32),
        lax.psum(grad_up.astype(jnp.bfloat16), "dp").astype(jnp.float32),
        lax.psum(grad_down.astype(jnp.bfloat16), "dp").astype(jnp.float32),
    )
    grad_class, grad_time, grad_ada, grad_qkv_weight, grad_proj, grad_up, grad_down = summed
    return (
        result.astype(jnp.bfloat16)[None],
        grad_input.astype(jnp.bfloat16)[None],
        grad_class,
        grad_time,
        grad_ada,
        grad_qkv_weight,
        grad_proj,
        grad_up,
        grad_down,
    )


def solution(mesh):
    return jax.shard_map(
        body,
        mesh=mesh,
        in_specs=(
            P("dp", "tensor", None),
            P("dp", None),
            P("dp", None),
            P("dp", None),
            P(),
            P(),
            P(None, "tensor"),
            P(None, None, "tensor"),
            P("tensor", None),
            P(None, "tensor"),
            P("tensor", None),
            P("dp", "tensor", None),
        ),
        out_specs=(
            P("dp", "tensor", None),
            P("dp", "tensor", None),
            P(),
            P(),
            P(None, "tensor"),
            P(None, None, "tensor"),
            P("tensor", None),
            P(None, "tensor"),
            P("tensor", None),
        ),
        check_vma=False,
    )
```

profile of v0, /device:TPU:0, one launch (start us, length us, event | category | flops | bytes accessed | tf_op | source)
XLA Modules:
  0.0 1208.8 jit_solution(14257579754387814371)
XLA Ops:
  11.9 3.9 fusion.65
  18.9 5.7 all_gather.15
  25.2 5.7 fusion.60
  31.0 5.3 copy-done.3
  38.2 37.7 %all-gather.5.cloned.1.call-done = bf16[1024,1152]{1,0:T(8,128)(2,1)} async-done(((bf16[512,1152]{1,0:T(8,128)(2,1)}), bf16[1024,1152]{1,0:T(8,128)(2,1)}) %all-gather.5.cloned.1.call-update) | async-done | bytes 2359312 | tf_op jit(solution)/shard_map/all_gather | solution.py:96
  75.9 7.6 convolution_convert_fusion.7
  86.5 39.1 %while.27 = (s32[]{:T(128)}, bf16[2,8,512,72]{2,3,1,0:T(8,128)(2,1)}, f32[2,8,512]{2,1,0:T(8,128)S(1)}, s32[2]{0:T(128)S(1)}, s32[1024]{0:T(1024)S(1)}, /*index=...) while((s32[]{:T(128)}, ...), condition=%wide.region_5.6_spmd, body=%wide.region_2.5_spmd.sunk | while | flops 1258811392 | bytes 70854920 | solution.py:126
  89.5 5.1 fusion.131
  94.6 4.5 fusion.132
  99.1 5.9 fusion.133
  109.0 5.1 fusion.131
  114.1 4.5 fusion.132
  118.7 5.9 fusion.133
  129.4 4.4 fusion.76
  133.8 60.1 %reduce-scatter.8.cloned.1.call-done = f32[512,1152]{1,0:T(8,128)} async-done(((f32[1024,1152]{1,0:T(8,128)}), f32[512,1152]{1,0:T(8,128)}) %reduce-scatter.8.cloned.1.call-update) | async-done | bytes 2359312 | tf_op jit(solution)/shard_map/reduce_scatter | solution.py:129
  193.9 3.1 fusion.74
  199.1 5.0 fusion.50
  204.2 8.7 all-gather.7.cloned.1.call-start
  213.0 27.5 %all-gather.9.cloned.1.call-done = bf16[1024,1152]{1,0:T(8,128)(2,1)} async-done(((bf16[512,1152]{1,0:T(8,128)(2,1)}), bf16[1024,1152]{1,0:T(8,128)(2,1)}) %all-gather.9.cloned.1.call-update) | async-done | bytes 2359312 | tf_op jit(solution)/shard_map/all_gather | solution.py:151
  240.4 11.6 fusion.77
  252.0 26.6 %all-gather.7.cloned.1.call-done = bf16[1024,1152]{1,0:T(8,128)(2,1)} async-done(((bf16[512,1152]{1,0:T(8,128)(2,1)}), bf16[1024,1152]{1,0:T(8,128)(2,1)}) %all-gather.7.cloned.1.call-update) | async-done | bytes 2359312 | tf_op jit(solution)/shard_map/all_gather | solution.py:138
  278.6 16.5 %fusion.31 = (bf16[1024,2304]{1,0:T(8,128)(2,1)S(1)}, f32[1024,2304]{1,0:T(8,128)}) fusion(f32[1024,2304]{1,0:T(8,128)} %fusion.77, bf16[1024,1152]{1,0:T(8,128)(2,1)} %all-gather.7.cloned.1.call-done, bf16[1152,2304]{1,0:T(8,128)(2,1)} %param.25), kind=kOutput, calls=%fused_computation.47 | convolution fusion | flops 5483003904 | bytes 31260672 | tf_op jit(solution)/shard_map/dot_general | solution.py:139
  297.3 10.4 fusion.78
  307.8 13.1 %convolution_convert_fusion.5 = bf16[1024,1152]{1,0:T(8,128)(2,1)} fusion(bf16[2304,1152]{1,0:T(8,128)(2,1)} %param.26, f32[1024,2304]{1,0:T(8,128)} %get-tuple-element.238), kind=kOutput, calls=%fused_computation.52 | convolution fusion | flops 5458231296 | bytes 17104896 | tf_op jit(solution)/shard_map/dot_general | solution.py:142
  321.4 46.5 %reduce-scatter.12.cloned.1.call-done = f32[512,1152]{1,0:T(8,128)} async-done(((f32[1024,1152]{1,0:T(8,128)}), f32[512,1152]{1,0:T(8,128)}) %reduce-scatter.12.cloned.1.call-update) | async-done | bytes 2359312 | tf_op jit(solution)/shard_map/reduce_scatter | solution.py:157
  367.9 3.8 fusion.73
  371.7 33.6 %reduce-scatter.10.cloned.1.call-done = bf16[512,1152]{1,0:T(8,128)(2,1)} async-done(((bf16[1024,1152]{1,0:T(8,128)(2,1)}), bf16[512,1152]{1,0:T(8,128)(2,1)}) %reduce-scatter.10.cloned.1.call-update) | async-done | bytes 1179664 | tf_op jit(solution)/shard_map/reduce_scatter | solution.py:141
  405.3 8.0 multiply_convert_fusion.2
  413.4 36.2 %all-gather.11.cloned.1.call-done = bf16[1024,1152]{1,0:T(8,128)(2,1)} async-done(((bf16[512,1152]{1,0:T(8,128)(2,1)}), bf16[1024,1152]{1,0:T(8,128)(2,1)}) %all-gather.11.cloned.1.call-update) | async-done | bytes 2359312 | tf_op jit(solution)/shard_map/all_gather | solution.py:163
  449.6 4.4 convolution_convert_fusion.12
  455.1 121.4 %while.28 = (s32[]{:T(128)}, f32[8,1024,72]{1,2,0:T(8,128)}, f32[8,1024,72]{1,2,0:T(8,128)}, bf16[2,8,512,72]{2,3,1,0:T(8,128)(2,1)}, s32[2]{0:T(128)S(1)}, /*in...) while((s32[]{:T(128)}, f32[8,1024,72]{1,2,0:T(8,128)}, ...), condition=%wide.region_15.16_spmd.clone, body=%wide.region_13.15_spmd.clone.sunk | while | flops 3061411840 | bytes 200632656 | solution.py:200
  458.1 9.9 fusion.143
  468.0 13.1 %multiply_reduce_fusion.4 = (f32[8,512]{1,0:T(8,128)S(1)}, f32[8,512,1024]{2,1,0:T(8,128)}) fusion(f32[8,512,1024]{2,1,0:T(8,128)} %fusion.143, f32[8,512]{1,0:T(8,128)S(1)} %constant_dynamic-slice_fusion.3, bf16[8,1024,72]{1,2,0:T(8,128)(2,1)S(1)} %get-tuple-element.451, bf16[8,1024,72]{1,2,0:T(8,128)(2,1)S(1)} %copy-done.5, s32[]{:T(128)S(6)} %select_n.47, ...), kind=kOutput, calls=%fused_computation.16.clone.1 | convolution fusion | flops 624947200 | bytes 35880964 | tf_op jit(solution)/shard_map/while/body/eval_jaxpr/hqd,hkd->hqk/dot_general | solution.py:111
  481.1 14.9 %multiply_convert_fusion.9 = bf16[8,512,1024]{2,1,0:T(8,128)(2,1)} fusion(f32[8,512,1024]{2,1,0:T(8,128)} %get-tuple-element.375, f32[8,512,1024]{2,1,0:T(8,128)} %fusion.143, f32[8,512]{1,0:T(8,128)S(1)} %get-tuple-element.376), kind=kLoop, calls=%fused_computation.15.clone.1 | loop fusion | flops 12582912 | bytes 41959424 | tf_op jit(solution)/shard_map/while/body/eval_jaxpr/convert_element_type | solution.py:179
  496.0 8.9 select_add_fusion.5
  504.9 7.0 fusion.144
  518.4 9.8 fusion.143
  528.2 13.1 %multiply_reduce_fusion.4 = (f32[8,512]{1,0:T(8,128)S(1)}, f32[8,512,1024]{2,1,0:T(8,128)}) fusion(f32[8,512,1024]{2,1,0:T(8,128)} %fusion.143, f32[8,512]{1,0:T(8,128)S(1)} %constant_dynamic-slice_fusion.3, bf16[8,1024,72]{1,2,0:T(8,128)(2,1)S(1)} %get-tuple-element.451, bf16[8,1024,72]{1,2,0:T(8,128)(2,1)S(1)} %copy-done.5, s32[]{:T(128)S(6)} %select_n.47, ...), kind=kOutput, calls=%fused_computation.16.clone.1 | convolution fusion | flops 624947200 | bytes 35880964 | tf_op jit(solution)/shard_map/while/body/eval_jaxpr/hqd,hkd->hqk/dot_general | solution.py:111
  541.3 14.9 %multiply_convert_fusion.9 = bf16[8,512,1024]{2,1,0:T(8,128)(2,1)} fusion(f32[8,512,1024]{2,1,0:T(8,128)} %get-tuple-element.375, f32[8,512,1024]{2,1,0:T(8,128)} %fusion.143, f32[8,512]{1,0:T(8,128)S(1)} %get-tuple-element.376), kind=kLoop, calls=%fused_computation.15.clone.1 | loop fusion | flops 12582912 | bytes 41959424 | tf_op jit(solution)/shard_map/while/body/eval_jaxpr/convert_element_type | solution.py:179
  556.2 9.7 select_add_fusion.5
  565.9 7.0 fusion.144
  576.5 3.6 copy.24
  580.1 4.0 stack_reshape.3
  584.1 2.5 maximum_convert_fusion
  588.4 6.3 convolution_convert_fusion.6
  596.3 9.8 convolution_convert_fusion.2
  606.2 11.5 convolution_convert_fusion.1
  617.7 6.3 convolution_convert_fusion.4
  623.9 5.7 reduce-scatter.14.cloned.1.call-done
  631.2 2.8 fusion.59
  634.3 3.8 multiply_dynamic-update-slice_fusion.1
  642.1 4.8 convolution_convert_fusion.3
  648.7 4.4 convolution_convert_fusion.9
  653.2 23.9 %reduce-scatter.16.cloned.1.call-done = bf16[3456,4]{1,0:T(8,128)(2,1)} async-done(((bf16[6912,4]{1,0:T(8,128)(2,1)}), bf16[3456,4]{1,0:T(8,128)(2,1)}) %reduce-scatter.16.cloned.1.call-update) | async-done | bytes 27664
  677.0 5.7 convolution_convert_fusion.11
  682.8 5.5 psum.56
  690.3 3.7 convolution_convert_fusion.8
  694.1 5.6 convolution_convert_fusion
  699.6 467.9 %all-reduce.3.cloned.1.call-done = (bf16[1001,1152]{1,0:T(8,128)(2,1)}, bf16[256,1152]{1,0:T(8,128)(2,1)}, bf16[1152,3456]{1,0:T(8,128)(2,1)}, bf16[1152,3,576]{...) async-done(((bf16[1001,1152]{1,0:T(8,128)(2,1)}, bf16[256,1152]{1,0:T(8,128)(2,1)}, ...) | async-done | bytes 26784016 | tf_op jit(solution)/shard_map/psum | solution.py:236
  1169.7 4.2 convert_element_type.180
  1177.0 4.6 convert_element_type.186
  1181.5 4.9 convert_element_type.190
  1186.5 4.8 convert_element_type.192
  1191.3 10.3 convert_element_type.184
  (202 shorter events, 54.5 us)
Async XLA Ops:
  7.2 122.2 %copy-start = (bf16[576,1152]{1,0:T(8,128)(2,1)S(1)}, bf16[576,1152]{1,0:T(8,128)(2,1)}, u32[]{:S(2)}) copy-start(bf16[576,1152]{1,0:T(8,128)(2,1)} %param.24) | copy-start | bytes 3981316
  7.2 4.7 copy-start.47
  7.2 68.7 %all-gather.5.cloned.1.call-start = ((), (), s32[]{:S(2)}) async-start(), calls=%async_computation.5 | async-start | bytes 3538944 | tf_op jit(solution)/shard_map/all_gather | solution.py:96
  8.0 9.7 copy-start.11
  9.7 21.3 %copy-start.39 = (f32[512]{0:T(512)}, f32[512]{0:T(512)S(1)}, u32[]{:S(2)}) copy-start(f32[512]{0:T(512)S(1)} %broadcast_multiply_fusion.5) | copy-start | bytes 6148
  11.7 19.2 %copy-start.41 = (f32[512]{0:T(512)}, f32[512]{0:T(512)S(1)}, u32[]{:S(2)}) copy-start(f32[512]{0:T(512)S(1)} %add_rsqrt_fusion.1) | copy-start | bytes 6148
  11.9 3.9 copy-start.43
  11.9 3.9 copy-start.45
  17.7 6.9 copy-start.30
  25.2 11.0 copy-start.12
  31.0 5.3 copy-start.3
  37.9 156.1 %reduce-scatter.8.cloned.1.call-start = ((), (), s32[]{:S(2)}) async-start(), calls=%async_computation.6 | async-start | bytes 7077888 | tf_op jit(solution)/shard_map/reduce_scatter | solution.py:129
  94.6 4.6 copy-start.4
  94.6 4.6 copy-start.21
  114.1 4.6 copy-start.4
  114.1 4.6 copy-start.21
  133.8 106.6 %all-gather.9.cloned.1.call-start = ((), (), s32[]{:S(2)}) async-start(), calls=%async_computation.9 | async-start | bytes 3538944 | tf_op jit(solution)/shard_map/all_gather | solution.py:151
  197.0 7.2 copy-start.6
  197.0 2.1 copy-start.15
  197.0 208.3 %copy-start.33 = (f32[512]{0:T(512)}, f32[512]{0:T(512)S(1)}, u32[]{:S(2)}) copy-start(f32[512]{0:T(512)S(1)} %broadcast_multiply_fusion.4) | copy-start | bytes 6148
  199.1 206.2 %copy-start.37 = (f32[512]{0:T(512)}, f32[512]{0:T(512)S(1)}, u32[]{:S(2)}) copy-start(f32[512]{0:T(512)S(1)} %add_rsqrt_fusion) | copy-start | bytes 6148
  204.2 74.4 %all-gather.7.cloned.1.call-start = ((), (), s32[]{:S(2)}) async-start(), calls=%async_computation.7 | async-start | bytes 3538944 | tf_op jit(solution)/shard_map/all_gather | solution.py:138
  212.9 155.0 %reduce-scatter.12.cloned.1.call-start = ((), (), s32[]{:S(2)}) async-start(), calls=%async_computation.10 | async-start | bytes 7077888 | tf_op jit(solution)/shard_map/reduce_scatter | solution.py:157
  295.1 2.2 copy-start.53
  307.7 97.6 %reduce-scatter.10.cloned.1.call-start = ((), (), s32[]{:S(2)}) async-start(), calls=%async_computation.8 | async-start | bytes 3538944 | tf_op jit(solution)/shard_map/reduce_scatter | solution.py:141
  320.9 128.7 %all-gather.11.cloned.1.call-start = ((), (), s32[]{:S(2)}) async-start(), calls=%async_computation.11 | async-start | bytes 3538944 | tf_op jit(solution)/shard_map/all_gather | solution.py:163
  413.3 216.2 %reduce-scatter.14.cloned.1.call-start = ((), (), s32[]{:S(2)}) async-start(), calls=%async_computation.12 | async-start | bytes 3538944 | tf_op jit(solution)/shard_map/reduce_scatter | solution.py:207
  458.1 9.9 copy-start.5
  504.9 7.0 copy-start.2
  504.9 7.0 copy-start.9
  518.4 9.8 copy-start.5
  565.9 7.0 copy-start.2
  565.9 7.0 copy-start.9
  576.4 7.6 copy-start.8
  584.1 4.3 copy-start.49
  586.6 1.8 copy-start.24
  594.7 1.7 copy-start.52
  594.7 82.4 %reduce-scatter.16.cloned.1.call-start = ((), (), s32[]{:S(2)}) async-start(), calls=%async_computation.13 | async-start | bytes 2654208
  596.3 9.8 copy-start.51
  606.2 11.5 copy-start.25
  606.2 11.5 copy-start.50
  623.9 7.2 copy-start.13
  623.9 7.2 copy-start.40
  623.9 7.2 copy-start.42
  631.2 2.9 copy-start.18
  631.2 3.1 copy-start.19
  634.3 3.8 copy-start.14
  638.1 1.7 copy-start.7
  638.1 1.7 copy-start.34
  638.1 1.7 copy-start.38
  646.9 1.8 copy-start.29
  648.7 518.9 %all-reduce.3.cloned.1.call-start = ((), (), s32[]{:S(2)}) async-start(), calls=%async_computation.14 | async-start | bytes 53600256 | tf_op jit(solution)/shard_map/psum | solution.py:236
  653.1 35.1 %copy-start.32 = (f32[4,1152]{1,0:T(4,128)S(1)}, f32[4,1152]{1,0:T(4,128)}, u32[]{:S(2)}) copy-start(f32[4,1152]{1,0:T(4,128)} %copy-done.31) | copy-start | bytes 55300
  653.1 35.1 %copy-start.44 = (f32[4,128]{1,0:T(4,128)S(1)}, f32[4,128]{1,0:T(4,128)}, u32[]{:S(2)}) copy-start(f32[4,128]{1,0:T(4,128)} %copy-done.43) | copy-start | bytes 6148
  653.1 35.1 %copy-start.46 = (f32[4,128]{1,0:T(4,128)S(1)}, f32[4,128]{1,0:T(4,128)}, u32[]{:S(2)}) copy-start(f32[4,128]{1,0:T(4,128)} %copy-done.45) | copy-start | bytes 6148
  653.1 37.2 %copy-start.48 = (s32[1,4]{1,0:T(1,128)S(1)}, s32[1,4]{1,0:T(1,128)}, u32[]{:S(2)}) copy-start(s32[1,4]{1,0:T(1,128)} %param.18) | copy-start | bytes 52
  682.8 11.3 copy-start.26
  1169.7 4.2 copy-start.27
  1173.9 3.1 copy-start.23
  1173.9 7.6 slice-start.2
  1177.0 4.6 slice-start.3
  1177.0 9.5 slice-start
  1181.5 4.9 slice-start.1
  1191.3 10.3 copy-start.1
  (11 other events, 12.8 us)
Sparse Core Ops, SparseCore 0:
  38.0 37.8 all-gather.4
  133.9 59.9 reduce-scatter.7
  204.3 36.0 all-gather.8
  242.5 36.0 all-gather.6
  307.9 59.9 reduce-scatter.11
  370.6 34.7 reduce-scatter.9
  413.5 36.0 all-gather.10
  594.8 34.7 reduce-scatter.13
  648.8 28.2 reduce-scatter.15
  699.8 467.7 all-reduce.2
where the time goes:
time: 1220 us; the launch traced here: 1210 us
  waiting for transfers between devices  766 us (63%)
  matrix products  245 us (20%)
  other arithmetic  111 us (9%)
  local copies, waits for them, and re-layouts  43.1 us (4%)
  between operations  15.1 us (1%)
    psum x1, waiting for transfers between devices, body(): lax.psum(grad_class.astype(jnp.bfloat16), 'dp').astype(jnp.float32)  468 us
    reduce_scatter x1, waiting for transfers between devices, body(): lax.psum_scatter(jnp.dot(attended, proj_weight, preferred_element_type=jn...  60.1 us
    reduce_scatter x1, waiting for transfers between devices, body(): lax.psum_scatter(times_transposed(grad_hidden, up_weight), 'tensor', scat...  46.5 us
    dot_general x5, matrix products, times_transposed(): lax.dot_general(left, right, (((1,), (1,)), ((), ())), preferred_element_...  38.4 us
    all_gather x1, waiting for transfers between devices, body(): inputs_one = lax.all_gather(modulated_one, 'tensor', axis=0, tiled=True)  37.7 us
    dot_general x5, matrix products, contract_rows(): lax.dot_general(left, right, (((0,), (0,)), ((), ())), preferred_element_...  37.5 us
    dot_general x4, matrix products, scores_of(): jnp.einsum('hqd,hkd->hqk', query_block, keys, preferred_element_type=jnp....  36.4 us
    all_gather x1, waiting for transfers between devices, body(): grads_one = lax.all_gather(grad_branch_one, 'tensor', axis=0, tiled=True)  36.2 us
  transfers between devices with their start and end apart: 10, of which 10 were waited for; matrix products, arithmetic and copies ran while one was open for 5% of the time, Pallas kernels for 0%

commit v1 on v0

v1 whole, which is shorter than its diff:
```python
import functools
import math

import jax
import jax.numpy as jnp
from jax import lax
from jax.experimental import pallas as pl
from jax.experimental.pallas import tpu as pltpu
from jax.sharding import PartitionSpec as P

HEAD_DIM = 72
SHORT = 256
HIGH = lax.Precision.HIGHEST
F32 = jnp.float32
BF16 = jnp.bfloat16
SCALE = 1.0 / math.sqrt(HEAD_DIM)
SCALE_LOG2 = SCALE * math.log2(math.e)


def dot(left, right, left_dim, right_dim, precision=None):
    return lax.dot_general(
        left,
        right,
        (((left_dim,), (right_dim,)), ((), ())),
        precision=precision,
        preferred_element_type=F32,
    )


def features(steps_f, width_total):
    half = width_total // 2
    freqs = jnp.exp(-math.log(10000.0) * jnp.arange(half, dtype=F32) / half)
    angles = steps_f[:, None] * freqs[None, :]
    return jnp.concatenate([jnp.cos(angles), jnp.sin(angles)], axis=1)


def normalize(values):
    average = jnp.mean(values, axis=-1, keepdims=True)
    centred = values - average
    inverse = lax.rsqrt(jnp.mean(centred * centred, axis=-1, keepdims=True) + 1e-06)
    return centred * inverse, inverse


def norm_back(grad_normed, normed, inverse):
    first = jnp.mean(grad_normed, axis=-1, keepdims=True)
    second = jnp.mean(grad_normed * normed, axis=-1, keepdims=True)
    return inverse * (grad_normed - first - normed * second)


def gelu_parts(x):
    root = math.sqrt(2.0 / math.pi)
    square = x * x
    bent = jnp.tanh(root * x * (1.0 + 0.044715 * square))
    half = 0.5 * (1.0 + bent)
    slope = half + 0.5 * x * (1.0 - bent * bent) * root * (1.0 + 3 * 0.044715 * square)
    return x * half, slope


def attend_kernel(block, q_ref, k_ref, v_ref, bias_ref, hot_ref, o_ref, lse_ref):
    tokens = q_ref.shape[2]
    query = jnp.concatenate([q_ref[0], bias_ref[...]], axis=0)
    key = jnp.concatenate([k_ref[0], hot_ref[...]], axis=0).T
    value = v_ref[0]
    for start in range(0, tokens, block):
        part = slice(start, start + block)
        scores = dot(key, query[:, part], 1, 0)
        top = jnp.max(scores, axis=0, keepdims=True) * SCALE_LOG2
        exps = jnp.exp2(scores * SCALE_LOG2 - top)
        total = jnp.sum(exps, axis=0, keepdims=True)
        out = dot(value, exps.astype(BF16), 1, 0)
        o_ref[0, :, part] = (out / total).astype(BF16)
        lse_ref[0, :, part] = top + jnp.log2(total)


def attend_back_kernel(
    block, q_ref, k_ref, v_ref, bias_ref, hot_ref, o_ref, do_ref, lse_ref, grad_ref
):
    tokens = q_ref.shape[2]
    query = jnp.concatenate([q_ref[0], bias_ref[...]], axis=0)
    key = jnp.concatenate([k_ref[0], hot_ref[...]], axis=0).T
    value = v_ref[0].T
    query_rows = q_ref[0].T
    grad_out = do_ref[0]
    grad_rows = grad_out.T
    delta = jnp.sum(grad_out.astype(F32) * o_ref[0].astype(F32), axis=0, keepdims=True)
    lse = lse_ref[0]
    grad_key = grad_value = None
    for start in range(0, tokens, block):
        part = slice(start, start + block)
        scores = dot(key, query[:, part], 1, 0)
        probs = jnp.exp2(scores * SCALE_LOG2 - lse[:, part])
        grad_probs = dot(value, grad_out[:, part], 1, 0)
        grad_scores = (probs * (grad_probs - delta[:, part])).astype(BF16)
        value_term = dot(probs.astype(BF16), grad_rows[part], 1, 0)
        key_term = dot(grad_scores, query_rows[part], 1, 0)
        grad_value = value_term if grad_value is None else grad_value + value_term
        grad_key = key_term if grad_key is None else grad_key + key_term
        grad_ref[0, 0, :, part] = (dot(k_ref[0], grad_scores, 1, 0) * SCALE).astype(BF16)
    grad_ref[1, 0] = (grad_key * SCALE).astype(BF16).T
    grad_ref[2, 0] = grad_value.astype(BF16).T


def head_spec(tokens, offset):
    return pl.BlockSpec((1, HEAD_DIM, tokens), lambda head: (head + offset, 0, 0))


def whole_spec(shape):
    return pl.BlockSpec(shape, lambda head: (0,) * len(shape))


def row_spec(tokens):
    return pl.BlockSpec((1, 1, tokens), lambda head: (head, 0, 0))


def attend(qkv, bias, hot, first, count):
    heads = qkv.shape[0] // 3
    tokens = qkv.shape[2]
    block = min(tokens, (1 << 20) // tokens)
    work = count * tokens * tokens
    return pl.pallas_call(
        functools.partial(attend_kernel, block),
        grid=(count,),
        in_specs=[
            head_spec(tokens, first),
            head_spec(tokens, heads + first),
            head_spec(tokens, 2 * heads + first),
            whole_spec(bias.shape),
            whole_spec(hot.shape),
        ],
        out_specs=[head_spec(tokens, 0), row_spec(tokens)],
        out_shape=[
            jax.ShapeDtypeStruct((count, HEAD_DIM, tokens), BF16),
            jax.ShapeDtypeStruct((count, 1, tokens), F32),
        ],
        compiler_params=pltpu.CompilerParams(vmem_limit_bytes=48 << 20),
        cost_estimate=pl.CostEstimate(
            flops=2400 * work, bytes_accessed=8 * count * HEAD_DIM * tokens, transcendentals=work
        ),
    )(qkv, qkv, qkv, bias, hot)


def attend_back(qkv, bias, hot, out, grad_out, lse, first, count):
    heads = qkv.shape[0] // 3
    tokens = qkv.shape[2]
    block = min(tokens, (1 << 19) // tokens)
    work = count * tokens * tokens
    return pl.pallas_call(
        functools.partial(attend_back_kernel, block),
        grid=(count,),
        in_specs=[
            head_spec(tokens, first),
            head_spec(tokens, heads + first),
            head_spec(tokens, 2 * heads + first),
            whole_spec(bias.shape),
            whole_spec(hot.shape),
            head_spec(tokens, first),
            head_spec(tokens, first),
            row_spec(tokens),
        ],
        out_specs=pl.BlockSpec((3, 1, HEAD_DIM, tokens), lambda head: (0, head, 0, 0)),
        out_shape=jax.ShapeDtypeStruct((3, count, HEAD_DIM, tokens), BF16),
        compiler_params=pltpu.CompilerParams(vmem_limit_bytes=56 << 20),
        cost_estimate=pl.CostEstimate(
            flops=3200 * work, bytes_accessed=16 * count * HEAD_DIM * tokens, transcendentals=work
        ),
    )(qkv, qkv, qkv, bias, hot, out, grad_out, lse)


def block_step(
    dp_size,
    tensor_size,
    tokens,
    segments,
    labels,
    timesteps,
    class_table,
    time_weight,
    ada_weight,
    qkv_weight,
    proj_weight,
    up_weight,
    down_weight,
    cotangent,
):
    pair = tensor_size == 2
    position = lax.axis_index("tensor")
    own_low = tokens[0]
    shard, width = own_low.shape
    pack = segments.shape[1]
    slot_count = labels.shape[1]
    class_count = class_table.shape[0]
    freq_width = time_weight.shape[0]
    local_width = qkv_weight.shape[2]
    heads = local_width // HEAD_DIM
    chunk = shard * SHORT // pack

    def swap(x):
        return lax.ppermute(x, "tensor", [(0, 1), (1, 0)])

    def gather(x, axis):
        if pair:
            return jnp.concatenate([x, swap(x)], axis=axis)
        return lax.all_gather(x, "tensor", axis=axis, tiled=True)

    def own_rows(x):
        if pair:
            return x[:shard]
        return lax.dynamic_slice_in_dim(x, position * shard, shard, 0)

    def summed_rows(make):
        if pair:
            away = make(shard, pack).astype(BF16)
            return make(0, shard) + swap(away).astype(F32)
        whole = make(0, pack).astype(BF16)
        return lax.psum_scatter(whole, "tensor", scatter_dimension=0, tiled=True).astype(F32)

    def across(x):
        if pair:
            return jnp.concatenate([swap(x[:, shard:]), swap(x[:, :shard])], axis=1)
        return lax.all_gather(x, "tensor", axis=0, tiled=True)

    def sum_dp(parts):
        return [lax.psum(p.astype(BF16), "dp").astype(F32) for p in parts]

    tokens_low = gather(own_low, 0)
    proj_all = gather(proj_weight, 0)
    grad_low = gather(cotangent[0], 0)
    labels_all = lax.all_gather(labels[0], "dp", axis=0, tiled=True)
    steps_all = lax.all_gather(timesteps[0], "dp", axis=0, tiled=True)

    seg = segments[0]
    if pair:
        seg = jnp.where(position == 0, seg, jnp.roll(seg, shard))
    chunk_seg = seg[::chunk]
    slots = jnp.arange(slot_count, dtype=jnp.int32)
    chunk_hot = (chunk_seg[:, None] == slots[None, :]).astype(F32)
    mask_rows = -(-slot_count // 8) * 8
    same = jnp.arange(mask_rows, dtype=jnp.int32)[:, None] == seg[None, :]
    hot = same.astype(BF16)
    bias = jnp.where(same, 0.0, -1e30).astype(BF16)

    rows = [lax.dynamic_slice_in_dim(class_table, labels[0, i], 1, 0) for i in range(slot_count)]
    condition = jnp.concatenate(rows, axis=0) + dot(
        features(timesteps[0].astype(F32), freq_width), time_weight, 1, 0, HIGH
    )
    act_low = jax.nn.silu(condition).astype(BF16)
    mod_part = dot(act_low, ada_weight, 1, 0)
    if pair:
        mod_away = swap(mod_part)
        modulation = jnp.where(
            position == 0,
            jnp.concatenate([mod_part, mod_away], axis=1),
            jnp.concatenate([mod_away, mod_part], axis=1),
        )
    else:
        modulation = lax.all_gather(mod_part, "tensor", axis=1, tiled=True)
    condition_all = lax.all_gather(condition, "dp", axis=0, tiled=True)
    per_chunk = dot(chunk_hot, modulation, 1, 0, HIGH)
    mods = [m[:, None, :] for m in jnp.split(per_chunk, 6, axis=1)]
    shift_one, scale_one, gate_one, shift_two, scale_two, gate_two = mods
    own_chunks = shard // chunk

    def chunked(x):
        return x.reshape(x.shape[0] // chunk, chunk, x.shape[1])

    def flat(x):
        return x.reshape(x.shape[0] * chunk, x.shape[2])

    def own_chunk(m):
        if pair:
            return m[:own_chunks]
        return lax.dynamic_slice_in_dim(m, position * own_chunks, own_chunks, 0)

    tokens_f = chunked(tokens_low.astype(F32))
    normed_one, _ = normalize(tokens_f)
    inputs_one = flat((normed_one * (1.0 + scale_one) + shift_one).astype(BF16))
    qkv_flat = qkv_weight.reshape(width, 3 * local_width)
    qkv = dot(qkv_flat, inputs_one, 0, 1).astype(BF16).reshape(3 * heads, HEAD_DIM, pack)
    out, lse = attend(qkv, bias, hot, 0, heads)
    out_flat = out.reshape(local_width, pack)
    out_other = across(out_flat)
    if pair:
        branch_one = dot(out_flat, proj_all[:local_width], 0, 0) + dot(
            out_other, proj_all[local_width:], 0, 0
        )
    else:
        branch_one = dot(out_other, proj_all, 0, 0)
    branch_one = chunked(branch_one)
    halfway = tokens_f + gate_one * branch_one
    normed_two, inverse_two = normalize(halfway)
    inputs_two = flat((normed_two * (1.0 + scale_two) + shift_two).astype(BF16))

    hidden = dot(inputs_two, up_weight, 1, 0)
    active, slope = gelu_parts(hidden)
    active = active.astype(BF16)
    slope = slope.astype(BF16)
    grad_branch_two = flat((chunked(grad_low.astype(F32)) * gate_two).astype(BF16))
    grad_down = dot(active, grad_branch_two, 0, 0)
    grad_active = dot(grad_branch_two, down_weight, 1, 1)
    grad_hidden = (grad_active * slope.astype(F32)).astype(BF16)
    grad_up = dot(inputs_two, grad_hidden, 0, 0)
    grad_mod_two = chunked(summed_rows(lambda a, b: dot(grad_hidden[a:b], up_weight, 1, 1)))
    branch_two = chunked(summed_rows(lambda a, b: dot(active[a:b], down_weight, 1, 0)))
    own_halfway = chunked(own_rows(flat(halfway)))
    own_branch_one = chunked(own_rows(flat(branch_one)))
    own_normed_two, own_inverse_two = normalize(own_halfway)
    grad_out = chunked(cotangent[0].astype(F32))
    result = own_halfway + own_chunk(gate_two) * branch_two
    grad_gate_two = grad_out * branch_two
    grad_halfway = grad_out + norm_back(
        grad_mod_two * (1.0 + own_chunk(scale_two)), own_normed_two, own_inverse_two
    )
    grad_gate_one = grad_halfway * own_branch_one
    grad_branch_one = flat((grad_halfway * own_chunk(gate_one)).astype(BF16))

    if pair:
        grad_att_own = dot(proj_all[:local_width], grad_branch_one, 1, 1).astype(BF16)
        grad_att_away = dot(proj_all[local_width:], grad_branch_one, 1, 1).astype(BF16)
        grad_att = jnp.concatenate([grad_att_own, swap(grad_att_away)], axis=1)
        grads_one = gather(grad_branch_one, 0)
    else:
        grads_one = gather(grad_branch_one, 0)
        grad_att = dot(proj_weight, grads_one, 1, 1).astype(BF16)
    grad_proj = dot(out_flat, grads_one, 1, 0)
    grad_qkv = attend_back(
        qkv, bias, hot, out, grad_att.reshape(heads, HEAD_DIM, pack), lse, 0, heads
    ).reshape(3 * local_width, pack)
    grad_qkv_weight = dot(inputs_one, grad_qkv, 0, 1).reshape(width, 3, local_width)
    grad_mod_one = chunked(summed_rows(lambda a, b: dot(grad_qkv[:, a:b], qkv_flat, 0, 1)))
    own_normed_one, own_inverse_one = normalize(chunked(own_low.astype(F32)))
    grad_input = grad_halfway + norm_back(
        grad_mod_one * (1.0 + own_chunk(scale_one)), own_normed_one, own_inverse_one
    )

    terms = [
        grad_mod_one,
        grad_mod_one * own_normed_one,
        grad_gate_one,
        grad_mod_two,
        grad_mod_two * own_normed_two,
        grad_gate_two,
    ]
    chunk_terms = jnp.concatenate([jnp.sum(t, axis=1) for t in terms], axis=1)
    slot_terms = dot(own_chunk(chunk_hot), chunk_terms, 0, 0, HIGH).astype(BF16)
    if pair:
        half = slot_terms.shape[1] // 2
        low, high = slot_terms[:, :half], slot_terms[:, half:]
        keep = jnp.where(position == 0, low, high)
        away = jnp.where(position == 0, high, low)
        grad_modulation = (keep.astype(F32) + swap(away).astype(F32)).astype(BF16)
    else:
        grad_modulation = lax.psum_scatter(
            slot_terms, "tensor", scatter_dimension=1, tiled=True
        )
    grad_mod_all = lax.all_gather(grad_modulation, "dp", axis=0, tiled=True)
    act_all = jax.nn.silu(condition_all).astype(BF16)
    grad_ada = dot(act_all, grad_mod_all, 0, 0)
    cond_part = dot(grad_mod_all, ada_weight, 1, 1).astype(BF16)
    if pair:
        grad_act = cond_part.astype(F32) + swap(cond_part).astype(F32)
    else:
        grad_act = lax.psum(cond_part, "tensor").astype(F32)
    grad_condition = jax.vjp(jax.nn.silu, condition_all)[1](grad_act)[0]
    classes = jnp.arange(class_count, dtype=jnp.int32)
    label_hot = (labels_all[:, None] == classes[None, :]).astype(F32)
    grad_class = dot(label_hot, grad_condition, 0, 0, HIGH)
    grad_time = dot(features(steps_all.astype(F32), freq_width), grad_condition, 0, 0, HIGH)

    grad_up, grad_down = sum_dp([grad_up, grad_down])
    last, grad_qkv_weight, _ = lax.optimization_barrier((grad_proj, grad_qkv_weight, grad_up[0, 0]))
    grad_proj, grad_qkv_weight = sum_dp([last, grad_qkv_weight])
    return (
        flat(result).astype(BF16)[None],
        flat(grad_input).astype(BF16)[None],
        grad_class,
        grad_time,
        grad_ada,
        grad_qkv_weight,
        grad_proj,
        grad_up,
        grad_down,
    )


def solution(mesh):
    return jax.shard_map(
        functools.partial(block_step, mesh.shape["dp"], mesh.shape["tensor"]),
        mesh=mesh,
        in_specs=(
            P("dp", "tensor", None),
            P("dp", None),
            P("dp", None),
            P("dp", None),
            P(),
            P(),
            P(None, "tensor"),
            P(None, None, "tensor"),
            P("tensor", None),
            P(None, "tensor"),
            P("tensor", None),
            P("dp", "tensor", None),
        ),
        out_specs=(
            P("dp", "tensor", None),
            P("dp", "tensor", None),
            P(),
            P(),
            P(None, "tensor"),
            P(None, None, "tensor"),
            P("tensor", None),
            P(None, "tensor"),
            P("tensor", None),
        ),
        check_vma=False,
    )
```

time: 1220 us -> 613 us (0.50)
  waiting for transfers between devices: 766 us -> 293 us
  matrix products: 245 us -> 129 us
  other arithmetic: 111 us -> 43.1 us
  blocking collectives: 11.2 us -> 60.6 us
  Pallas kernels: 0 us -> 38.3 us
  local copies, waits for them, and re-layouts: 43.1 us -> 5.53 us
    psum x1, waiting for transfers between devices: 468 us -> 201 us  [sum_dp(): return [lax.psum(p.astype(BF16), 'dp').astype(F32) for p in parts]]
    reduce_scatter x4 -> x0, waiting for transfers between devices: 146 us -> none  [the longest x1 60.1 us: body(): lax.psum_scatter(jnp.dot(attended, proj_weight, preferred_element_type=jn...]
    all_gather x4 -> x0, waiting for transfers between devices: 128 us -> none  [the longest x1 37.7 us: body(): inputs_one = lax.all_gather(modulated_one, 'tensor', axis=0, tiled=True)]
    dot_general x35 -> x25, matrix products: 245 us -> 129 us  [dot(): lax.dot_general(left, right, (((left_dim,), (right_dim,)), ((), ())), pre...]
    ppermute x0 -> x13, waiting for transfers between devices: none -> 92.3 us  [swap(): return lax.ppermute(x, 'tensor', [(0, 1), (1, 0)])]
    convert_element_type x14, other arithmetic: 80.2 us -> 30.5 us  [the longest x4 17.5 us: sum_dp(): return [lax.psum(p.astype(BF16), 'dp').astype(F32) for p in parts]]
    all_gather x1 -> x2, blocking collectives: 5.75 us -> 47.4 us  [the longest x1 26.3 us: block_step(): condition_all = lax.all_gather(condition, 'dp', axis=0, tiled=True)]
    pallas_call x0 -> x2, Pallas kernels: none -> 38.3 us  [the longest x1 24.1 us: attend_back(): pl.pallas_call(functools.partial(attend_back_kernel, block), grid=(count,...]
  transfers between devices with their start and end apart: 10 -> 14, of which waited for: 10 -> 8; matrix products, arithmetic and copies ran while one was open for 5% -> 16% of each run, Pallas kernels for 0% -> 6%
where the time goes in v1:
time: 613 us; the launch traced here: 608 us
  waiting for transfers between devices  293 us (48%)
  matrix products  129 us (21%)
  blocking collectives  60.6 us (10%)
  other arithmetic  43.1 us (7%)
  Pallas kernels  38.3 us (6%)
  between operations  23.7 us (4%)
  starting transfers between devices  15.2 us (2%)
    psum x1, waiting for transfers between devices, sum_dp(): return [lax.psum(p.astype(BF16), 'dp').astype(F32) for p in parts]  201 us
    dot_general x25, matrix products, dot(): lax.dot_general(left, right, (((left_dim,), (right_dim,)), ((), ())), pre...  129 us
    ppermute x13, waiting for transfers between devices, swap(): return lax.ppermute(x, 'tensor', [(0, 1), (1, 0)])  92.3 us
    all_gather x1, blocking collectives, block_step(): condition_all = lax.all_gather(condition, 'dp', axis=0, tiled=True)  26.3 us
    pallas_call x1, Pallas kernels, attend_back(): pl.pallas_call(functools.partial(attend_back_kernel, block), grid=(count,...  24.1 us
    all_gather x1, blocking collectives, block_step(): grad_mod_all = lax.all_gather(grad_modulation, 'dp', axis=0, tiled=True)  21.1 us
    convert_element_type x4, other arithmetic, sum_dp(): return [lax.psum(p.astype(BF16), 'dp').astype(F32) for p in parts]  17.5 us
    ppermute x13, starting transfers between devices, swap(): return lax.ppermute(x, 'tensor', [(0, 1), (1, 0)])  15.1 us
  transfers between devices with their start and end apart: 14, of which 8 were waited for; matrix products, arithmetic and copies ran while one was open for 16% of the time, Pallas kernels for 6%

profile of v1, /device:TPU:0, one launch (start us, length us, event | category | flops | bytes accessed | tf_op | source)
XLA Modules:
  0.0 608.3 jit_solution(13556818935058938210)
XLA Ops:
  7.3 0.7 convert_bitcast_fusion
  8.0 1.4 fusion.73
  17.3 0.9 constant_dynamic-slice_fusion.3
  18.2 0.7 convolution_add_fusion.1
  18.9 4.5 fusion.49
  23.4 3.0 collective-permute-start.1
  26.5 1.9 collective-permute-start
  30.1 0.8 convert_reduce_fusion.1
  30.9 13.2 %all-reduce.2 = (s32[64]{0:T(128)}, s32[64]{0:T(128)S(1)}) all-reduce(s32[64]{0:T(128)S(1)} %bitcast_dynamic-update-slice_fusion.1, s32[64]{0:T(128)S(1)} %bitcast_dynamic-update-slice_fusion), channel_id=2, replica_groups=mesh['dp'=16,'tensor'=2] {'dp'}, use_global_device_ids=true, to_apply=%add | all-reduce | flops 128 | bytes 1024
  45.7 35.1 %collective-permute-done = bf16[512,1152]{1,0:T(8,128)(2,1)S(1)} collective-permute-done((bf16[512,1152]{1,0:T(8,128)(2,1)S(1)}, bf16[512,1152]{1,0:T(8,128)(2,1)S(1)}, u32[]{:S(2)}, u32[]{:S(2)}) %collective-permute-start) | collective-permute-done | bytes 1179680 | tf_op jit(solution)/shard_map/ppermute | solution.py:198
  81.2 0.8 multiply_reduce_fusion.1
  82.0 2.0 add_convert_fusion.1
  84.1 5.0 convolution_convert_fusion.3
  89.2 14.2 %shard_map.187 = (bf16[8,72,1024]{2,1,0:T(8,128)(2,1)S(1)}, f32[8,1,1024]{2,1,0:T(1,128)S(1)}) custom-call(bf16[24,72,1024]{2,1,0:T(8,128)(2,1)S(1)} %bitcast.144, bf16[24,72,1024]{2,1,0:T(8,128)(2,1)S(1)} %bitcast.145, bf16[24,72,1024]{2,1,0:T(8,128)(2,1)S(1)} %bitcast.146, bf16[8,1024]{1,0:T(8,128)(2,1)S(1)} %select_convert_fusion.bias_ref, ...), custom_call_target="tpu_custom_call" | custom-call | flops 20132659200 | bytes 4718592 | tf_op jit(solution)/shard_map/pallas_call | solution.py:120
  103.5 1.0 collective-permute-start.2
  104.5 1.1 collective-permute-start.3
  105.6 3.5 fusion.74
  109.5 12.4 %collective-permute-done.2 = bf16[576,512]{1,0:T(8,128)(2,1)S(1)} collective-permute-done((bf16[576,512]{1,0:T(8,128)(2,1)S(1)}, bf16[576,512]{1,0:T(8,128)(2,1)S(1)}, u32[]{:S(2)}, u32[]{:S(2)}) %collective-permute-start.2) | collective-permute-done | bytes 589856 | tf_op jit(solution)/shard_map/ppermute | solution.py:198
  121.9 11.1 %collective-permute-done.3 = bf16[576,512]{1,0:T(8,128)(2,1)S(1)} collective-permute-done((bf16[576,512]{1,0:T(8,128)(2,1)S(1)}, bf16[576,512]{1,0:T(8,128)(2,1)S(1)}, u32[]{:S(2)}, u32[]{:S(2)}) %collective-permute-start.3) | collective-permute-done | bytes 589856 | tf_op jit(solution)/shard_map/ppermute | solution.py:198
  133.0 4.5 fusion.25
  137.5 4.7 fusion
  142.3 2.7 fusion.1
  145.0 10.0 %multiply_convert_fusion.1 = (bf16[1024,2304]{1,0:T(8,128)(2,1)}, f32[1024,2304]{1,0:T(8,128)}) fusion(bf16[1024,1152]{1,0:T(8,128)(2,1)S(1)} %fusion.1, bf16[1152,2304]{1,0:T(8,128)(2,1)S(1)} %bitcast.164), kind=kOutput, calls=%fused_computation.4 | convolution fusion | flops 5457051648 | bytes 21823488 | tf_op jit(solution)/shard_map/dot_general | solution.py:21
  155.0 12.4 %multiply_convert_fusion = bf16[1024,2304]{1,0:T(8,128)(2,1)S(1)} fusion(bf16[1024,1152]{1,0:T(8,128)(2,1)S(1)} %get-tuple-element.77, bf16[2304,1152]{1,0:T(8,128)(2,1)} %param.22, f32[1024,2304]{1,0:T(8,128)} %get-tuple-element.75), kind=kOutput, calls=%fused_computation.2 | convolution fusion | flops 5483003904 | bytes 21823488 | tf_op jit(solution)/shard_map/dot_general | solution.py:21
  167.4 4.3 convolution_convert_fusion.5
  171.7 1.2 collective-permute-start.7
  172.9 10.0 %convolution_convert_fusion = bf16[2304,1152]{1,0:T(8,128)(2,1)} fusion(bf16[1024,2304]{1,0:T(8,128)(2,1)} %get-tuple-element.74, bf16[1024,1152]{1,0:T(8,128)(2,1)S(1)} %get-tuple-element.77), kind=kOutput, calls=%fused_computation | convolution fusion | flops 5438472192 | bytes 12386304 | tf_op jit(solution)/shard_map/dot_general | solution.py:21
  183.0 4.9 convolution_convert_fusion.6
  187.9 0.9 collective-permute-start.5
  189.6 11.2 %collective-permute-done.7 = bf16[512,1152]{1,0:T(8,128)(2,1)S(1)} collective-permute-done((bf16[512,1152]{1,0:T(8,128)(2,1)}, bf16[512,1152]{1,0:T(8,128)(2,1)S(1)}, u32[]{:S(2)}, u32[]{:S(2)}) %collective-permute-start.7) | collective-permute-done | bytes 1179680 | tf_op jit(solution)/shard_map/ppermute | solution.py:198
  200.8 3.4 fusion.14
  204.2 1.7 fusion.16
  205.9 17.8 %collective-permute-done.5 = bf16[512,1152]{1,0:T(8,128)(2,1)S(1)} collective-permute-done((bf16[512,1152]{1,0:T(8,128)(2,1)S(1)}, bf16[512,1152]{1,0:T(8,128)(2,1)S(1)}, u32[]{:S(2)}, u32[]{:S(2)}) %collective-permute-start.5) | collective-permute-done | bytes 1179680 | tf_op jit(solution)/shard_map/ppermute | solution.py:198
  223.7 6.8 %fusion.3 = (f32[4,1152]{1,0:T(4,128)}, f32[512,1152]{1,0:T(8,128)S(1)}) fusion(bf16[4,128,1152]{2,1,0:T(8,128)(2,1)} %bitcast.47, bf16[512,1152]{1,0:T(8,128)(2,1)S(1)} %collective-permute-done.5, bf16[2304,1152]{1,0:T(8,128)(2,1)} %param.22, bf16[1024,2304]{1,0:T(8,128)(2,1)S(1)} %bitcast.195), kind=kOutput, calls=%fused_computation.26 | convolution fusion | flops 2720853504 | bytes 12404736 | tf_op jit(solution)/shard_map/dot_general | solution.py:21
  230.5 3.9 multiply_reduce_fusion.2
  234.6 2.4 fusion.24
  237.0 1.7 collective-permute-start.8
  238.7 7.6 %convolution_convert_fusion.1 = bf16[1152,2304]{1,0:T(8,128)(2,1)} fusion(bf16[1024,1152]{1,0:T(8,128)(2,1)S(1)} %copy-done.15, bf16[1024,2304]{1,0:T(8,128)(2,1)S(1)} %bitcast.176), kind=kOutput, calls=%fused_computation.1 | convolution fusion | flops 5438472192 | bytes 12386304 | tf_op jit(solution)/shard_map/dot_general | solution.py:21
  246.8 2.3 fusion.23
  249.1 4.3 collective-permute-done.8
  253.4 1.2 pad_maximum_fusion.1
  254.5 24.1 %shard_map.188 = bf16[3,8,72,1024]{3,2,1,0:T(8,128)(2,1)} custom-call(bf16[24,72,1024]{2,1,0:T(8,128)(2,1)} %bitcast.147, bf16[24,72,1024]{2,1,0:T(8,128)(2,1)} %bitcast.148, bf16[24,72,1024]{2,1,0:T(8,128)(2,1)} %bitcast.149, bf16[8,1024]{1,0:T(8,128)(2,1)} %copy-done.5, bf16[8,1024]{1,0:T(8,128)(2,1)} %copy-done.4, bf16[8,72,1024]{2,1,0:T(8,128)(2,1)} %copy-done.2, ...), custom_call_target="tpu_custom_call" | custom-call | flops 26843545600 | bytes 9437184 | tf_op jit(solution)/shard_map/pallas_call | solution.py:147
  278.7 9.2 %fusion.75 = bf16[1152,3,576]{0,2,1:T(8,128)(2,1)} fusion(bf16[1024,1152,1]{1,0,2:T(8,128)(2,1)S(1)} %bitcast.173, bf16[3,576,1024]{2,1,0:T(8,128)(2,1)} %bitcast.183), kind=kOutput, calls=%fused_computation.168 | convolution fusion | flops 4076863488 | bytes 9879552 | tf_op jit(solution)/shard_map/dot_general | solution.py:21
  287.9 4.0 fusion.10
  292.0 6.3 %convolution_convert_fusion.4 = bf16[512,1152]{1,0:T(8,128)(2,1)} fusion(bf16[1152,1728]{0,1:T(8,128)(2,1)} %bitcast.169, bf16[1728,1024]{1,0:T(8,128)(2,1)} %bitcast.184), kind=kOutput, calls=%fused_computation.21 | convolution fusion | flops 2039021568 | bytes 6930432 | tf_op jit(solution)/shard_map/dot_general | solution.py:21
  298.3 1.6 collective-permute-start.9
  299.9 26.3 %all-gather.3 = f32[16,4,1152]{2,1,0:T(4,128)} all-gather(f32[1,4,1152]{2,1,0:T(4,128)S(1)} %bitcast.186), channel_id=1, replica_groups=mesh['dp'=16,'tensor'=2] {'dp'}, dimensions={0}, use_global_device_ids=true | all-gather | bytes 313344 | tf_op jit(solution)/shard_map/all_gather | solution.py:257
  326.2 1.8 reshape.419
  328.5 0.8 multiply_cosine_fusion
  329.4 6.1 %fusion.15 = (f32[4,1152]{1,0:T(4,128)S(1)}, f32[4,1152]{1,0:T(4,128)S(1)}, f32[4,128,1152]{2,1,0:T(8,128)S(1)}, f32[512,1152]{1,0:T(8,128)S(1)}) fusion(f32[4,128]{1,0:T(4,128)S(1)} %get-tuple-element.63, f32[4,128]{1,0:T(4,128)S(1)} %get-tuple-element.61, bf16[4,128,1152]{2,1,0:T(8,128)(2,1)S(1)} %bitcast.158, ...), kind=kOutput, calls=%fused_computation.45 | convolution fusion | flops 2043141120 | bytes 12869632 | tf_op jit(solution)/shard_map/dot_general | solution.py:21
  335.9 0.9 collective-permute-start.10
  336.8 0.9 fusion.17
  337.7 1.9 add_convert_fusion.2
  339.9 21.1 %all-gather.2 = bf16[16,4,3456]{2,1,0:T(4,128)(2,1)S(1)} all-gather(bf16[1,4,3456]{2,1,0:T(4,128)(2,1)S(1)} %fusion.47), channel_id=1, replica_groups=mesh['dp'=16,'tensor'=2] {'dp'}, dimensions={0}, use_global_device_ids=true | all-gather | bytes 470016 | tf_op jit(solution)/shard_map/all_gather | solution.py:355
  361.1 5.9 convolution_convert_fusion.7
  367.0 1.2 collective-permute-start.11
  368.3 8.2 %fusion.32 = f32[1152,3456]{1,0:T(8,128)} fusion(bf16[64,3456]{1,0:T(8,128)(2,1)S(1)} %reshape.417, f32[64,1152]{1,0:T(8,128)S(1)} %copy-done.11), kind=kOutput, calls=%fused_computation.85 | convolution fusion | flops 509976576 | bytes 16662528 | tf_op jit(solution)/shard_map/dot_general | solution.py:21
  376.5 2.2 fusion.41
  378.6 4.3 fusion.31
  382.9 200.6 %all-reduce.6.cloned.1.call-done = (bf16[1152,3,576]{0,2,1:T(8,128)(2,1)}, bf16[576,1152]{1,0:T(8,128)(2,1)}, bf16[1152,2304]{1,0:T(8,128)(2,1)}, bf16[2304,1152]{1,0:T(8,128)(2,1)}) async-done(((bf16[1152,3,576]{0,2,1:T(8,128)(2,1)}, bf16[576,1152]{1,0:T(8,128)(2,1)}, bf16[1152,2304]{1,0:T(8,128)(2,1)}, bf16[2304,1152]{1,0:T(8,128)(2,1)}), (bf16[1152,3,576]{0,2,1:T(8,128)(2,1)}, ...) | async-done | bytes 15925264 | tf_op jit(solution)/shard_map/psum | solution.py:223
  583.5 3.2 convert_element_type.274
  586.7 4.6 convert_element_type.272
  591.2 4.9 convert_element_type.276
  596.2 4.8 convert_element_type.278
  (173 shorter events, 6.6 us)
Async XLA Ops:
  7.2 11.0 %copy-start = (f32[256,1152]{1,0:T(8,128)S(1)}, f32[256,1152]{1,0:T(8,128)}, u32[]{:S(2)}) copy-start(f32[256,1152]{1,0:T(8,128)} %param.17) | copy-start | bytes 3538948
  7.2 576.3 %all-reduce.6.cloned.1.call-start = ((), (), s32[]{:S(2)}) async-start(), calls=%async_computation | async-start | bytes 31850496 | tf_op jit(solution)/shard_map/psum | solution.py:223
  7.3 16.1 %copy-start.34 = (f32[128]{0:T(128)}, f32[128]{0:T(128)S(1)}, u32[]{:S(2)}) copy-start(f32[128]{0:T(128)S(1)} %multiply_exponential_fusion) | copy-start | bytes 1540
  18.8 4.5 copy-start.19
  18.8 7.7 %copy-start.8 = (bf16[1,512,1152]{2,1,0:T(8,128)(2,1)S(1)}, bf16[1,512,1152]{2,1,0:T(8,128)(2,1)}, u32[]{:S(2)}) copy-start(bf16[1,512,1152]{2,1,0:T(8,128)(2,1)} %param.12) | copy-start | bytes 3538948
  18.8 9.7 %copy-start.28 = (s32[1,1024]{1,0:T(1,128)S(1)}, s32[1,1024]{1,0:T(1,128)}, u32[]{:S(2)}) copy-start(s32[1,1024]{1,0:T(1,128)} %param.13) | copy-start | bytes 12292
  18.9 9.7 %copy-start.41 = (u32[32]{0:T(128)S(1)}, u32[32]{0:T(128)}, u32[]{:S(2)}) copy-start(u32[32]{0:T(128)} %constant.60) | copy-start | bytes 388
  18.9 11.0 %copy-start.33 = (s32[1,4]{1,0:T(1,128)S(1)}, s32[1,4]{1,0:T(1,128)}, u32[]{:S(2)}) copy-start(s32[1,4]{1,0:T(1,128)} %param.14) | copy-start | bytes 52
  18.9 11.1 %copy-start.38 = (s32[1,4]{1,0:T(1,128)S(1)}, s32[1,4]{1,0:T(1,128)}, u32[]{:S(2)}) copy-start(s32[1,4]{1,0:T(1,128)} %param.15) | copy-start | bytes 52
  23.4 21.3 %collective-permute-start.1 = (f32[4,3456]{1,0:T(4,128)S(1)}, f32[4,3456]{1,0:T(4,128)S(1)}, u32[]{:S(2)}, u32[]{:S(2)}) collective-permute-start(f32[4,3456]{1,0:T(4,128)S(1)} %fusion.49), channel_id=1, source_target_pairs={{0,1},{1,0},{2,3},{3,2},{4,5},{5,4},{6,7},{7,6},{8,9},{9,8},{10,11... | collective-permute-start | bytes 165896 | tf_op jit(solution)/shard_map/ppermute | solution.py:198
  26.4 111.1 %collective-permute-start.6 = (bf16[512,1152]{1,0:T(8,128)(2,1)}, bf16[512,1152]{1,0:T(8,128)(2,1)}, u32[]{:S(2)}, u32[]{:S(2)}) collective-permute-start(bf16[512,1152]{1,0:T(8,128)(2,1)} %bitcast.25), channel_id=1, source_target_pairs={{0,1},{1,0},{2,3},{3,2},{4,5},{5,4},{6,7},{7,6},{8,9},{9,8},{10,11... | collective-permute-start | bytes 3538952 | tf_op jit(solution)/shard_map/ppermute | solution.py:198
  26.5 54.3 %collective-permute-start = (bf16[512,1152]{1,0:T(8,128)(2,1)S(1)}, bf16[512,1152]{1,0:T(8,128)(2,1)S(1)}, u32[]{:S(2)}, u32[]{:S(2)}) collective-permute-start(bf16[512,1152]{1,0:T(8,128)(2,1)S(1)} %bitcast.150), channel_id=1, source_target_pairs={{0,1},{1,0},{2,3},{3,2},{4,5},{5,4},{6,7},{7,6},{8,9},{9,8},{10,11... | collective-permute-start | bytes 3538952 | tf_op jit(solution)/shard_map/ppermute | solution.py:198
  28.4 81.0 %collective-permute-start.4 = (bf16[576,1152]{1,0:T(8,128)(2,1)}, bf16[576,1152]{1,0:T(8,128)(2,1)}, u32[]{:S(2)}, u32[]{:S(2)}) collective-permute-start(bf16[576,1152]{1,0:T(8,128)(2,1)} %param.20), channel_id=1, source_target_pairs={{0,1},{1,0},{2,3},{3,2},{4,5},{5,4},{6,7},{7,6},{8,9},{9,8},{10,11... | collective-permute-start | bytes 3981320 | tf_op jit(solution)/shard_map/ppermute | solution.py:198
  28.6 60.6 %copy-start.4 = (bf16[8,1024]{1,0:T(8,128)(2,1)}, bf16[8,1024]{1,0:T(8,128)(2,1)S(1)}, u32[]{:S(2)}) copy-start(bf16[8,1024]{1,0:T(8,128)(2,1)S(1)} %fusion.46.hot_ref) | copy-start | bytes 49156
  28.6 60.6 %copy-start.5 = (bf16[8,1024]{1,0:T(8,128)(2,1)}, bf16[8,1024]{1,0:T(8,128)(2,1)S(1)}, u32[]{:S(2)}) copy-start(bf16[8,1024]{1,0:T(8,128)(2,1)S(1)} %select_convert_fusion.bias_ref) | copy-start | bytes 49156
  44.7 37.3 %copy-start.39 = (s32[8]{0:T(128)}, s32[8]{0:T(128)S(1)}, u32[]{:S(2)}) copy-start(s32[8]{0:T(128)S(1)} %slice.94) | copy-start | bytes 100
  45.6 143.1 %copy-start.21 = (f32[4,1152]{1,0:T(4,128)}, f32[4,1152]{1,0:T(4,128)S(1)}, u32[]{:S(2)}) copy-start(f32[4,1152]{1,0:T(4,128)S(1)} %get-tuple-element.47) | copy-start | bytes 55300
  45.6 158.6 %copy-start.17 = (f32[4,1152]{1,0:T(4,128)}, f32[4,1152]{1,0:T(4,128)S(1)}, u32[]{:S(2)}) copy-start(f32[4,1152]{1,0:T(4,128)S(1)} %get-tuple-element.48) | copy-start | bytes 55300
  84.0 5.1 copy-start.12
  89.1 14.3 %copy-start.6 = (bf16[1024,1728]{0,1:T(8,128)(2,1)}, bf16[1024,1728]{0,1:T(8,128)(2,1)S(1)}, u32[]{:S(2)}) copy-start(bf16[1024,1728]{0,1:T(8,128)(2,1)S(1)} %convolution_convert_fusion.3) | copy-start | bytes 10616836
  103.4 5.7 copy-start.2
  103.4 5.7 copy-start.7
  103.5 18.4 %collective-permute-start.2 = (bf16[576,512]{1,0:T(8,128)(2,1)S(1)}, bf16[576,512]{1,0:T(8,128)(2,1)S(1)}, u32[]{:S(2)}, u32[]{:S(2)}) collective-permute-start(bf16[576,512]{1,0:T(8,128)(2,1)S(1)} %get-tuple-element.44), channel_id=1, source_target_pairs={{0,1},{1,0},{2,3},{3,2},{4,5},{5,4},{6,7},{7,6},{8,9},{9,8},{10,11... | collective-permute-start | bytes 1769480 | tf_op jit(solution)/shard_map/ppermute | solution.py:198
  104.5 28.5 %collective-permute-start.3 = (bf16[576,512]{1,0:T(8,128)(2,1)S(1)}, bf16[576,512]{1,0:T(8,128)(2,1)S(1)}, u32[]{:S(2)}, u32[]{:S(2)}) collective-permute-start(bf16[576,512]{1,0:T(8,128)(2,1)S(1)} %get-tuple-element.45), channel_id=1, source_target_pairs={{0,1},{1,0},{2,3},{3,2},{4,5},{5,4},{6,7},{7,6},{8,9},{9,8},{10,11... | collective-permute-start | bytes 1769480 | tf_op jit(solution)/shard_map/ppermute | solution.py:198
  133.0 12.0 %slice-start = ((s8[5308416]{0:T(1024)(128)(4,1)}), s8[4194304]{0:T(1024)(128)(4,1)S(1)}, s32[]{:S(2)}) async-start(s8[5308416]{0:T(1024)(128)(4,1)} %bitcast.163), calls=%async_computation.1 | async-start | bytes 8388608
  137.5 7.5 %slice-start.1 = ((s8[5308416]{0:T(1024)(128)(4,1)}), s8[1114112]{0:T(1024)(128)(4,1)S(1)}, s32[]{:S(2)}) async-start(s8[5308416]{0:T(1024)(128)(4,1)} %bitcast.163), calls=%async_computation.2 | async-start | bytes 2228224
  145.0 10.0 %copy-start.14 = (bf16[1024,1152]{1,0:T(8,128)(2,1)}, bf16[1024,1152]{1,0:T(8,128)(2,1)S(1)}, u32[]{:S(2)}) copy-start(bf16[1024,1152]{1,0:T(8,128)(2,1)S(1)} %fusion.1) | copy-start | bytes 7077892
  167.4 4.3 copy-start.16
  167.4 15.5 %slice-start.8 = ((s8[5308416]{0:T(1024)(128)(4,1)}), s8[4194304]{0:T(1024)(128)(4,1)S(1)}, s32[]{:S(2)}) async-start(s8[5308416]{0:T(1024)(128)(4,1)} %bitcast.192), calls=%async_computation.9 | async-start | bytes 8388608
  171.7 29.1 %collective-permute-start.7 = (bf16[512,1152]{1,0:T(8,128)(2,1)}, bf16[512,1152]{1,0:T(8,128)(2,1)S(1)}, u32[]{:S(2)}, u32[]{:S(2)}) collective-permute-start(bf16[512,1152]{1,0:T(8,128)(2,1)} %convolution_convert_fusion.5), channel_id=1, source_target_pairs={{0,1},{1,0},{2,3},{3,2},{4,5},{5,4},{6,7},{7,6},{8,9},{9,8},{10,11... | collective-permute-start | bytes 3538952 | tf_op jit(solution)/shard_map/ppermute | solution.py:198
  172.9 10.0 %slice-start.9 = ((s8[5308416]{0:T(1024)(128)(4,1)}), s8[1114112]{0:T(1024)(128)(4,1)S(1)}, s32[]{:S(2)}) async-start(s8[5308416]{0:T(1024)(128)(4,1)} %bitcast.192), calls=%async_computation.10 | async-start | bytes 2228224
  187.9 35.7 %collective-permute-start.5 = (bf16[512,1152]{1,0:T(8,128)(2,1)S(1)}, bf16[512,1152]{1,0:T(8,128)(2,1)S(1)}, u32[]{:S(2)}, u32[]{:S(2)}) collective-permute-start(bf16[512,1152]{1,0:T(8,128)(2,1)S(1)} %convolution_convert_fusion.6), channel_id=1, source_target_pairs={{0,1},{1,0},{2,3},{3,2},{4,5},{5,4},{6,7},{7,6},{8,9},{9,8},{10,11... | collective-permute-start | bytes 3538952 | tf_op jit(solution)/shard_map/ppermute | solution.py:198
  188.8 12.0 %slice-start.6 = ((s8[4718592]{0:T(1024)(128)(4,1)}), s8[4194304]{0:T(1024)(128)(4,1)S(1)}, s32[]{:S(2)}) async-start(s8[4718592]{0:T(1024)(128)(4,1)} %bitcast.175), calls=%async_computation.7 | async-start | bytes 8388608
  188.8 12.0 %slice-start.7 = ((s8[4718592]{0:T(1024)(128)(4,1)}), s8[524288]{0:T(1024)(128)(4,1)S(1)}, s32[]{:S(2)}) async-start(s8[4718592]{0:T(1024)(128)(4,1)} %bitcast.175), calls=%async_computation.8 | async-start | bytes 1048576
  189.2 34.5 %slice-start.10 = ((s8[4718592]{0:T(1024)(128)(4,1)}), s8[4194304]{0:T(1024)(128)(4,1)S(1)}, s32[]{:S(2)}) async-start(s8[4718592]{0:T(1024)(128)(4,1)} %bitcast.194), calls=%async_computation.11 | async-start | bytes 8388608
  200.8 22.8 %slice-start.11 = ((s8[4718592]{0:T(1024)(128)(4,1)}), s8[524288]{0:T(1024)(128)(4,1)S(1)}, s32[]{:S(2)}) async-start(s8[4718592]{0:T(1024)(128)(4,1)} %bitcast.194), calls=%async_computation.12 | async-start | bytes 1048576
  223.6 6.8 %copy-start.18 = (f32[4,1152]{1,0:T(4,128)S(1)}, f32[4,1152]{1,0:T(4,128)}, u32[]{:S(2)}) copy-start(f32[4,1152]{1,0:T(4,128)} %copy-done.17) | copy-start | bytes 55300
  223.7 6.8 %copy-start.24 = (f32[4,1152]{1,0:T(4,128)S(1)}, f32[4,1152]{1,0:T(4,128)}, u32[]{:S(2)}) copy-start(f32[4,1152]{1,0:T(4,128)} %get-tuple-element.49) | copy-start | bytes 55300
  237.0 16.3 %collective-permute-start.8 = (bf16[576,512]{1,0:T(8,128)(2,1)S(1)}, bf16[576,512]{1,0:T(8,128)(2,1)S(1)}, u32[]{:S(2)}, u32[]{:S(2)}) collective-permute-start(bf16[576,512]{1,0:T(8,128)(2,1)S(1)} %fusion.24), channel_id=1, source_target_pairs={{0,1},{1,0},{2,3},{3,2},{4,5},{5,4},{6,7},{7,6},{8,9},{9,8},{10,11... | collective-permute-start | bytes 1769480 | tf_op jit(solution)/shard_map/ppermute | solution.py:198
  246.3 41.5 %collective-permute-start.12 = (bf16[512,1152]{1,0:T(8,128)(2,1)S(1)}, bf16[512,1152]{1,0:T(8,128)(2,1)}, u32[]{:S(2)}, u32[]{:S(2)}) collective-permute-start(bf16[512,1152]{1,0:T(8,128)(2,1)S(1)} %bitcast.178), channel_id=1, source_target_pairs={{0,1},{1,0},{2,3},{3,2},{4,5},{5,4},{6,7},{7,6},{8,9},{9,8},{10,11... | collective-permute-start | bytes 3538952 | tf_op jit(solution)/shard_map/ppermute | solution.py:198
  254.5 24.1 %copy-start.13 = (bf16[8,128,1152]{2,1,0:T(8,128)(2,1)S(1)}, bf16[8,128,1152]{2,1,0:T(8,128)(2,1)}, u32[]{:S(2)}) copy-start(bf16[8,128,1152]{2,1,0:T(8,128)(2,1)} %copy-done.12) | copy-start | bytes 7077892
  278.7 9.2 %copy-start.3 = (bf16[8,72,1024]{2,1,0:T(8,128)(2,1)S(1)}, bf16[8,72,1024]{2,1,0:T(8,128)(2,1)}, u32[]{:S(2)}) copy-start(bf16[8,72,1024]{2,1,0:T(8,128)(2,1)} %copy-done.2) | copy-start | bytes 3538948
  291.9 7.9 %copy-start.20 = (f32[4,1152]{1,0:T(4,128)S(1)}, f32[4,1152]{1,0:T(4,128)}, u32[]{:S(2)}) copy-start(f32[4,1152]{1,0:T(4,128)} %copy-done.19) | copy-start | bytes 55300
  291.9 36.0 %copy-start.32 = (f32[512]{0:T(512)S(1)}, f32[512]{0:T(512)}, u32[]{:S(2)}) copy-start(f32[512]{0:T(512)} %convert_reduce_fusion.1) | copy-start | bytes 6148
  292.0 36.4 %copy-start.40 = (s32[8]{0:T(128)S(1)}, s32[8]{0:T(128)}, u32[]{:S(2)}) copy-start(s32[8]{0:T(128)} %copy-done.39) | copy-start | bytes 100
  292.0 36.5 %copy-start.35 = (f32[128]{0:T(128)S(1)}, f32[128]{0:T(128)}, u32[]{:S(2)}) copy-start(f32[128]{0:T(128)} %copy-done.34) | copy-start | bytes 1540
  292.0 36.5 %copy-start.36 = (f32[64]{0:T(128)S(1)}, f32[64]{0:T(128)}, u32[]{:S(2)}) copy-start(f32[64]{0:T(128)} %convert_element_type.284) | copy-start | bytes 772
  298.3 31.1 %collective-permute-start.9 = (bf16[512,1152]{1,0:T(8,128)(2,1)}, bf16[512,1152]{1,0:T(8,128)(2,1)}, u32[]{:S(2)}, u32[]{:S(2)}) collective-permute-start(bf16[512,1152]{1,0:T(8,128)(2,1)} %convolution_convert_fusion.4), channel_id=1, source_target_pairs={{0,1},{1,0},{2,3},{3,2},{4,5},{5,4},{6,7},{7,6},{8,9},{9,8},{10,11... | collective-permute-start | bytes 3538952 | tf_op jit(solution)/shard_map/ppermute | solution.py:198
  329.3 6.2 %copy-start.25 = (f32[4,1152]{1,0:T(4,128)S(1)}, f32[4,1152]{1,0:T(4,128)}, u32[]{:S(2)}) copy-start(f32[4,1152]{1,0:T(4,128)} %get-tuple-element.32) | copy-start | bytes 55300
  329.3 6.2 %copy-start.27 = (f32[4,1152]{1,0:T(4,128)S(1)}, f32[4,1152]{1,0:T(4,128)}, u32[]{:S(2)}) copy-start(f32[4,1152]{1,0:T(4,128)} %get-tuple-element.21) | copy-start | bytes 55300
  329.3 6.2 %copy-start.26 = (f32[4,1152]{1,0:T(4,128)S(1)}, f32[4,1152]{1,0:T(4,128)}, u32[]{:S(2)}) copy-start(f32[4,1152]{1,0:T(4,128)} %get-tuple-element.19) | copy-start | bytes 55300
  329.3 6.3 %copy-start.31 = (f32[4,1152]{1,0:T(4,128)S(1)}, f32[4,1152]{1,0:T(4,128)}, u32[]{:S(2)}) copy-start(f32[4,1152]{1,0:T(4,128)} %get-tuple-element.30) | copy-start | bytes 55300
  329.3 7.5 %copy-start.23 = (f32[4,1152]{1,0:T(4,128)S(1)}, f32[4,1152]{1,0:T(4,128)}, u32[]{:S(2)}) copy-start(f32[4,1152]{1,0:T(4,128)} %get-tuple-element.46) | copy-start | bytes 55300
  335.9 3.9 collective-permute-start.10
  361.1 7.2 %copy-start.11 = (f32[64,1152]{1,0:T(8,128)S(1)}, f32[64,1152]{1,0:T(8,128)}, u32[]{:S(2)}) copy-start(f32[64,1152]{1,0:T(8,128)} %reshape.419) | copy-start | bytes 884740
  367.0 9.5 %copy-start.29 = (f32[64,128]{1,0:T(8,128)S(1)}, f32[64,128]{1,0:T(8,128)}, u32[]{:S(2)}) copy-start(f32[64,128]{1,0:T(8,128)} %get-tuple-element.64) | copy-start | bytes 98308
  367.0 9.5 %copy-start.30 = (f32[64,128]{1,0:T(8,128)S(1)}, f32[64,128]{1,0:T(8,128)}, u32[]{:S(2)}) copy-start(f32[64,128]{1,0:T(8,128)} %get-tuple-element.65) | copy-start | bytes 98308
  367.0 11.6 %copy-start.37 = (s32[64]{0:T(128)S(1)}, s32[64]{0:T(128)}, u32[]{:S(2)}) copy-start(s32[64]{0:T(128)} %get-tuple-element.24) | copy-start | bytes 772
  367.0 9.4 %collective-permute-start.11 = (bf16[64,1152]{1,0:T(8,128)(2,1)S(1)}, bf16[64,1152]{1,0:T(8,128)(2,1)S(1)}, u32[]{:S(2)}, u32[]{:S(2)}) collective-permute-start(bf16[64,1152]{1,0:T(8,128)(2,1)S(1)} %convolution_convert_fusion.7), channel_id=1, source_target_pairs={{0,1},{1,0},{2,3},{3,2},{4,5},{5,4},{6,7},{7,6},{8,9},{9,8},{10,11... | collective-permute-start | bytes 442376 | tf_op jit(solution)/shard_map/ppermute | solution.py:198
  583.5 7.7 %slice-start.4 = ((s8[5308416]{0:T(1024)(128)(4,1)}), s8[4194304]{0:T(1024)(128)(4,1)S(1)}, s32[]{:S(2)}) async-start(s8[5308416]{0:T(1024)(128)(4,1)} %bitcast.167), calls=%async_computation.5 | async-start | bytes 8388608
  586.7 4.6 slice-start.5
  586.7 9.5 %slice-start.2 = ((s8[5308416]{0:T(1024)(128)(4,1)}), s8[4194304]{0:T(1024)(128)(4,1)S(1)}, s32[]{:S(2)}) async-start(s8[5308416]{0:T(1024)(128)(4,1)} %bitcast.165), calls=%async_computation.3 | async-start | bytes 8388608
  591.2 4.9 slice-start.3
  596.2 4.8 copy-start.1
  (4 other events, 13.3 us)
Sparse Core Ops, SparseCore 0:
  292.1 291.3 all-reduce.5

commit v2 on v0

--- a/solution.py
+++ b/solution.py
@@ -1,28 +1,56 @@
+import functools
 import math
 
 import jax
 import jax.numpy as jnp
 from jax import lax
+from jax.experimental import pallas as pl
+from jax.experimental.pallas import tpu as pltpu
 from jax.sharding import PartitionSpec as P
 
 HEAD_DIM = 72
-
-
+SHORT = 256
 HIGH = lax.Precision.HIGHEST
+F32 = jnp.float32
+BF16 = jnp.bfloat16
+SCALE = 1.0 / math.sqrt(HEAD_DIM)
+SCALE_LOG2 = SCALE * math.log2(math.e)
+
+
+def dot(left, right, left_dim, right_dim, precision=None):
+    return lax.dot_general(
+        left,
+        right,
+        (((left_dim,), (right_dim,)), ((), ())),
+        precision=precision,
+        preferred_element_type=F32,
+    )
 
 
 def features(steps_f, width_total):
     half = width_total // 2
-    freqs = jnp.exp(-math.log(10000.0) * jnp.arange(half, dtype=jnp.float32) / half)
+    freqs = jnp.exp(-math.log(10000.0) * jnp.arange(half, dtype=F32) / half)
     angles = steps_f[:, None] * freqs[None, :]
     return jnp.concatenate([jnp.cos(angles), jnp.sin(angles)], axis=1)
+
+
+def contract_rows(left, right):
+    return dot(left, right, 0, 0)
+
+
+def contract_exact(left, right):
+    return dot(left, right, 0, 0, HIGH)
+
+
+def times_transposed(left, right):
+    return dot(left, right, 1, 1)
 
 
 def normalize(values):
     average = jnp.mean(values, axis=-1, keepdims=True)
     centred = values - average
     inverse = lax.rsqrt(jnp.mean(centred * centred, axis=-1, keepdims=True) + 1e-06)
-    return (centred * inverse, inverse)
+    return centred * inverse, inverse
 
 
 def norm_back(grad_normed, normed, inverse):
@@ -31,25 +59,624 @@
     return inverse * (grad_normed - first - normed * second)
 
 
-def contract_rows(left, right):
-    return lax.dot_general(
-        left, right, (((0,), (0,)), ((), ())), preferred_element_type=jnp.float32
-    )
-
-
-def contract_exact(left, right):
-    return lax.dot_general(
-        left, right, (((0,), (0,)), ((), ())), precision=HIGH, preferred_element_type=jnp.float32
-    )
-
-
-def times_transposed(left, right):
-    return lax.dot_general(
-        left, right, (((1,), (1,)), ((), ())), preferred_element_type=jnp.float32
-    )
-
-
-def body(
+def gelu_parts(x):
+    root = math.sqrt(2.0 / math.pi)
+    square = x * x
+    bent = jnp.tanh(root * x * (1.0 + 0.044715 * square))
+    half = 0.5 * (1.0 + bent)
+    slope = half + 0.5 * x * (1.0 - bent * bent) * root * (1.0 + 3 * 0.044715 * square)
+    return x * half, slope
+
+
+def joined(own, other):
+    return jnp.concatenate([own[0], other[0]], axis=1)
+
+
+def attend_kernel(block, q0, q1, k0, k1, v0, v1, bias_ref, hot_ref, o_ref, lse_ref):
+    tokens = o_ref.shape[2]
+    query = jnp.concatenate([joined(q0, q1), bias_ref[...]], axis=0)
+    key = jnp.concatenate([joined(k0, k1), hot_ref[...]], axis=0).T
+    value = joined(v0, v1)
+    for start in range(0, tokens, block):
+        part = slice(start, start + block)
+        scores = dot(key, query[:, part], 1, 0)
+        top = jnp.max(scores, axis=0, keepdims=True) * SCALE_LOG2
+        exps = jnp.exp2(scores * SCALE_LOG2 - top)
+        total = jnp.sum(exps, axis=0, keepdims=True)
+        out = dot(value, exps.astype(BF16), 1, 0)
+        o_ref[0, :, part] = (out / total).astype(BF16)
+        lse_ref[0, :, part] = top + jnp.log2(total)
+
+
+def attend_back_kernel(
+    block, q0, q1, k0, k1, v0, v1, bias_ref, hot_ref, o_ref, do0, do1, lse_ref, grad_ref
+):
+    tokens = o_ref.shape[2]
+    query_all, key_all = joined(q0, q1), joined(k0, k1)
+    query = jnp.concatenate([query_all, bias_ref[...]], axis=0)
+    key = jnp.concatenate([key_all, hot_ref[...]], axis=0).T
+    value = joined(v0, v1).T
+    query_rows = query_all.T
+    grad_out = joined(do0, do1)
+    grad_rows = grad_out.T
+    delta = jnp.sum(grad_out.astype(F32) * o_ref[0].astype(F32), axis=0, keepdims=True)
+    lse = lse_ref[0]
+    grad_key = grad_value = None
+    for start in range(0, tokens, block):
+        part = slice(start, start + block)
+        scores = dot(key, query[:, part], 1, 0)
+        probs = jnp.exp2(scores * SCALE_LOG2 - lse[:, part])
+        grad_probs = dot(value, grad_out[:, part], 1, 0)
+        grad_scores = (probs * (grad_probs - delta[:, part])).astype(BF16)
+        value_term = dot(probs.astype(BF16), grad_rows[part], 1, 0)
+        key_term = dot(grad_scores, query_rows[part], 1, 0)
+        grad_value = value_term if grad_value is None else grad_value + value_term
+        grad_key = key_term if grad_key is None else grad_key + key_term
+        grad_ref[0, 0, :, part] = (dot(key_all, grad_scores, 1, 0) * SCALE).astype(BF16)
+    grad_ref[1, 0] = (grad_key * SCALE).astype(BF16).T
+    grad_ref[2, 0] = grad_value.astype(BF16).T
+
+
+def head_spec(tokens, offset):
+    return pl.BlockSpec((1, HEAD_DIM, tokens), lambda head: (head + offset, 0, 0))
+
+
+def whole_spec(shape):
+    return pl.BlockSpec(shape, lambda head: (0,) * len(shape))
+
+
+def row_spec(tokens):
+    return pl.BlockSpec((1, 1, tokens), lambda head: (head, 0, 0))
+
+
+SMALL = pl.CostEstimate(flops=1 << 20, bytes_accessed=1 << 20, transcendentals=0)
+
+
+def attend(own, other, bias, hot, first, count):
+    heads = own.shape[0] // 3
+    part = own.shape[2]
+    tokens = part + other.shape[2]
+    in_specs = [
+        head_spec(part, component * heads + first) for component in range(3) for _ in range(2)
+    ]
+    return pl.pallas_call(
+        functools.partial(attend_kernel, min(tokens, (1 << 20) // tokens)),
+        grid=(count,),
+        in_specs=in_specs + [whole_spec(bias.shape), whole_spec(hot.shape)],
+        out_specs=[head_spec(tokens, 0), row_spec(tokens)],
+        out_shape=[
+            jax.ShapeDtypeStruct((count, HEAD_DIM, tokens), BF16),
+            jax.ShapeDtypeStruct((count, 1, tokens), F32),
+        ],
+        compiler_params=pltpu.CompilerParams(vmem_limit_bytes=48 << 20),
+        cost_estimate=SMALL,
+    )(own, other, own, other, own, other, bias, hot)
+
+
+def attend_back(own, other, bias, hot, out, grad_own, grad_other, lse, first, count):
+    heads = own.shape[0] // 3
+    part = own.shape[2]
+    tokens = part + other.shape[2]
+    in_specs = [
+        head_spec(part, component * heads + first) for component in range(3) for _ in range(2)
+    ]
+    return pl.pallas_call(
+        functools.partial(attend_back_kernel, min(tokens, (1 << 19) // tokens)),
+        grid=(count,),
+        in_specs=in_specs
+        + [
+            whole_spec(bias.shape),
+            whole_spec(hot.shape),
+            head_spec(tokens, 0),
+            head_spec(part, first),
+            head_spec(part, first),
+            row_spec(tokens),
+        ],
+        out_specs=pl.BlockSpec((3, 1, HEAD_DIM, tokens), lambda head: (0, head, 0, 0)),
+        out_shape=jax.ShapeDtypeStruct((3, count, HEAD_DIM, tokens), BF16),
+        compiler_params=pltpu.CompilerParams(vmem_limit_bytes=56 << 20),
+        cost_estimate=SMALL,
+    )(own, other, own, other, own, other, bias, hot, out, grad_own, grad_other, lse)
+
+
+def write_kernel(place, blocks, aliased, *refs):
+    me = lax.axis_index("dp")
+    sources = refs[: len(refs) - 3 - aliased]
+    out_ref, wide, sems = refs[-3:]
+    copies = []
+    for group, source in enumerate(sources):
+        for block in range(blocks):
+            slot = group * blocks + block
+            wide[slot] = source[block].astype(F32)
+            copies.append(
+                pltpu.make_async_copy(
+                    wide.at[slot], place(out_ref, me, group, block), sems.at[slot]
+                )
+            )
+            copies[-1].start()
+    for copy in copies:
+        copy.wait()
+
+
+def write_out(groups, place, shape, onto=None):
+    blocks, rows, columns = groups[0].shape
+    count = len(groups) * blocks
+    anywhere = pl.BlockSpec(memory_space=pl.ANY)
+    extra = [] if onto is None else [onto]
+    return pl.pallas_call(
+        functools.partial(write_kernel, place, blocks, len(extra)),
+        in_specs=[pl.BlockSpec(memory_space=pltpu.VMEM)] * len(groups) + [anywhere] * len(extra),
+        out_specs=anywhere,
+        scratch_shapes=[
+            pltpu.VMEM((count, rows, columns), F32),
+            pltpu.SemaphoreType.DMA((count,)),
+        ],
+        out_shape=jax.ShapeDtypeStruct(shape, F32),
+        input_output_aliases={} if onto is None else {len(groups): 0},
+        compiler_params=pltpu.CompilerParams(vmem_limit_bytes=32 << 20),
+        cost_estimate=SMALL,
+    )(*groups, *extra)
+
+
+def pair_body(
+    tokens,
+    segments,
+    labels,
+    timesteps,
+    class_table,
+    time_weight,
+    ada_weight,
+    qkv_weight,
+    proj_weight,
+    up_weight,
+    down_weight,
+    cotangent,
+):
+    position = lax.axis_index("tensor")
+    rank = lax.axis_index("dp")
+    dp_size = 16
+    core, line, deep = rank % 2, rank // 2 % 2, rank // 4 % 2
+    own_low = tokens[0]
+    cot_low = cotangent[0]
+    shard, width = own_low.shape
+    pack = segments.shape[1]
+    slot_count = labels.shape[1]
+    class_count = class_table.shape[0]
+    freq_width = time_weight.shape[0]
+    local_width = qkv_weight.shape[2]
+    heads = local_width // HEAD_DIM
+    half_heads = heads // 2
+    half_width = local_width // 2
+    hidden_width = up_weight.shape[1]
+    chunk = shard * SHORT // pack
+    own_chunks = shard // chunk
+    CORE, LINE, DEEP, FAR = 1, 2, 4, 8
+
+    def fence(*values):
+        return lax.optimization_barrier(values)
+
+    def swap(x):
+        return lax.ppermute(x, "tensor", [(0, 1), (1, 0)])
+
+    def trade(x, bits):
+        return lax.ppermute(x, "dp", [(i, i ^ bits) for i in range(dp_size)])
+
+    def rows_of(x, index, count):
+        size = x.shape[0] // count
+        return lax.dynamic_slice_in_dim(x, index * size, size, 0)
+
+    def columns_of(x, index, count):
+        size = x.shape[1] // count
+        return lax.dynamic_slice_in_dim(x, index * size, size, 1)
+
+    def plus(a, b):
+        return (a.astype(F32) + b.astype(F32)).astype(BF16)
+
+    def halve(x, digit, bits):
+        return plus(rows_of(x, digit, 2), trade(rows_of(x, 1 - digit, 2), bits))
+
+    def gather_dp(x):
+        y = x[None]
+        y = jnp.concatenate([y, trade(y, CORE)], axis=0)
+        y = jnp.concatenate([y, trade(y, LINE)], axis=0)
+        y = jnp.concatenate([y, trade(y, DEEP), trade(y, FAR), trade(y, DEEP + FAR)], axis=0)
+        return y.reshape((dp_size * x.shape[0],) + x.shape[1:])
+
+    def chunked(x):
+        return x.reshape(x.shape[0] // chunk, chunk, x.shape[1])
+
+    def flat(x):
+        return x.reshape(x.shape[0] * chunk, x.shape[2])
+
+    quarter = shard // 2
+    cuts = (0, shard // 4, shard * 5 // 8, shard)
+    pieces = [own_low[a:b] for a, b in zip(cuts[:-1], cuts[1:], strict=True)]
+    arrived = [swap(pieces[0])]
+    ids = jnp.stack([labels[0], timesteps[0]], axis=1)
+
+    seg = segments[0]
+    seg = jnp.where(position == 0, seg, jnp.roll(seg, shard))
+    slots = jnp.arange(slot_count, dtype=jnp.int32)
+    chunk_hot = (seg[::chunk][:, None] == slots[None, :]).astype(F32)
+    mask_rows = -(-slot_count // 8) * 8
+    same = jnp.arange(mask_rows, dtype=jnp.int32)[:, None] == seg[None, :]
+    hot = same.astype(BF16)
+    bias = jnp.where(same, 0.0, -1e30).astype(BF16)
+
+    classes = jnp.arange(class_count, dtype=jnp.int32)
+
+    def condition_of(ids):
+        label_hot = (ids[:, 0][:, None] == classes[None, :]).astype(F32)
+        feats = features(ids[:, 1].astype(F32), freq_width)
+        values = dot(label_hot, class_table, 1, 0, HIGH) + dot(feats, time_weight, 1, 0, HIGH)
+        return label_hot, feats, values
+
+    condition, arrived[0], pieces[1] = fence(condition_of(ids)[2], arrived[0], pieces[1])
+    arrived.append(swap(pieces[1]))
+    act_low = jax.nn.silu(condition).astype(BF16)
+    mod_part, arrived[1], pieces[2] = fence(
+        dot(act_low, ada_weight, 1, 0), arrived[1], pieces[2]
+    )
+    arrived.append(swap(pieces[2]))
+    mod_away = swap(mod_part)
+    modulation = jnp.where(
+        position == 0,
+        jnp.concatenate([mod_part, mod_away], axis=1),
+        jnp.concatenate([mod_away, mod_part], axis=1),
+    )
+    per_chunk = dot(chunk_hot, modulation, 1, 0, HIGH)
+    mods_own = [m[:, None, :] for m in jnp.split(per_chunk[:own_chunks], 6, axis=1)]
+    mods_other = [m[:, None, :] for m in jnp.split(per_chunk[own_chunks:], 6, axis=1)]
+
+    weight_t = qkv_weight.transpose(1, 2, 0).reshape(3 * local_width, width)
+
+    def enter(low, mods):
+        values = chunked(low.astype(F32))
+        normed, inverse = normalize(values)
+        inputs = flat((normed * (1.0 + mods[1]) + mods[0]).astype(BF16))
+        return values, normed, inverse, inputs
+
+    def project(inputs):
+        return dot(weight_t, inputs, 1, 1).astype(BF16).reshape(3 * heads, HEAD_DIM, shard)
+
+    tokens_own, normed_one, inverse_one, inputs_one_own = enter(own_low, mods_own)
+    qkv_own = project(inputs_one_own)
+    arrived[2], proj_half, qkv_own = fence(arrived[2], rows_of(proj_weight, core, 2), qkv_own)
+    tokens_away = jnp.concatenate(arrived, axis=0)
+    proj_half = swap(proj_half)
+    tokens_other, normed_one_other, _, inputs_one_other = enter(tokens_away, mods_other)
+    qkv_other = project(inputs_one_other)
+    out_a, lse_a = attend(qkv_own, qkv_other, bias, hot, 0, half_heads)
+    out_a, qkv_own = fence(out_a, qkv_own)
+    away_a = swap(out_a.reshape(half_width, pack))
+    out_b, lse_b = attend(qkv_own, qkv_other, bias, hot, half_heads, half_heads)
+    out_b, proj_half, ids = fence(out_b, proj_half, ids)
+    away_b = swap(out_b.reshape(half_width, pack))
+    ids_all = gather_dp(ids)
+    proj_rest = trade(proj_half, CORE)
+    proj_other = jnp.where(
+        core == 0,
+        jnp.concatenate([proj_half, proj_rest], axis=0),
+        jnp.concatenate([proj_rest, proj_half], axis=0),
+    )
+    out_flat = jnp.concatenate([out_a, out_b], axis=0).reshape(local_width, pack)
+    own_part, other_part = slice(0, shard), slice(shard, pack)
+
+    def reordered(away):
+        return jnp.concatenate([away[:, other_part], away[:, own_part]], axis=1)
+
+    away_a, ids_all, proj_other = fence(away_a, ids_all, proj_other)
+    label_hot, features_all, condition_all = condition_of(ids_all)
+    first = dot(
+        jnp.concatenate([out_flat, reordered(away_a)], axis=0),
+        jnp.concatenate([proj_weight, proj_other[:half_width]], axis=0),
+        0,
+        0,
+    )
+    away_b, cot_a, cot_b, condition_all, first = fence(
+        away_b, cot_low[:quarter], cot_low[quarter:], condition_all, first
+    )
+    cot_away_a = swap(cot_a)
+    branch_one = first + dot(reordered(away_b), proj_other[half_width:], 0, 0)
+    branch_own, branch_other = branch_one[own_part], branch_one[other_part]
+
+    def middle(values, branch, mods):
+        halfway = values + mods[2] * chunked(branch)
+        normed, inverse = normalize(halfway)
+        inputs = flat((normed * (1.0 + mods[4]) + mods[3]).astype(BF16))
+        return halfway, normed, inverse, inputs
+
+    halfway, normed_two, inverse_two, inputs_two_own = middle(tokens_own, branch_own, mods_own)
+    _, normed_two_other, _, inputs_two_other = middle(tokens_other, branch_other, mods_other)
+    inputs_two = jnp.concatenate([inputs_two_own, inputs_two_other], axis=0)
+    inputs_two, cot_away_a, cot_b = fence(inputs_two, cot_away_a, cot_b)
+    cot_away_b = swap(cot_b)
+
+    hidden = dot(inputs_two, up_weight, 1, 0)
+    active, slope = gelu_parts(hidden)
+    active = active.astype(BF16)
+    slope = slope.astype(BF16)
+    active, slope, cot_away_b = fence(active, slope, cot_away_b)
+    cot_away = jnp.concatenate([cot_away_a, cot_away_b], axis=0)
+    grad_branch_two = jnp.concatenate(
+        [
+            flat((chunked(cot_low.astype(F32)) * mods_own[5]).astype(BF16)),
+            flat((chunked(cot_away.astype(F32)) * mods_other[5]).astype(BF16)),
+        ],
+        axis=0,
+    )
+
+    def down_half(half):
+        return dot(columns_of(active, half, 2), grad_branch_two, 0, 0)
+
+    down_away = trade(down_half(1 - core).astype(BF16), CORE)
+    grad_active = dot(grad_branch_two, down_weight, 1, 1)
+    grad_hidden = (grad_active * slope.astype(F32)).astype(BF16)
+    down_sum = plus(down_half(core), down_away)
+    down_sum, grad_hidden = fence(down_sum, grad_hidden)
+    down_x = trade(rows_of(down_sum, 1 - line, 2), LINE)
+    mod_two_other = dot(grad_hidden[other_part], up_weight, 1, 1)
+    mod_two_away = mod_two_other.astype(BF16)
+    mod_two_away, grad_hidden = fence(mod_two_away, grad_hidden)
+
+    def up_half(half):
+        return dot(inputs_two, columns_of(grad_hidden, half, 2), 0, 0)
+
+    arrived_a = swap(mod_two_away[:quarter])
+    up_away = trade(up_half(1 - core).astype(BF16), CORE)
+    up_sum = plus(up_half(core), up_away)
+    arrived_a, up_sum, mod_two_next, grad_hidden, active = fence(
+        arrived_a, up_sum, mod_two_away[quarter:], grad_hidden, active
+    )
+    arrived_b = swap(mod_two_next)
+    up_x = trade(rows_of(up_sum, 1 - line, 2), LINE)
+    mod_two = dot(grad_hidden[own_part], up_weight, 1, 1)
+    branch_two_away = dot(active[other_part], down_weight, 1, 0)
+    branch_two = dot(active[own_part], down_weight, 1, 0)
+    arrived_b, mod_two, branch_two_away, branch_two, down_x = fence(
+        arrived_b, mod_two, branch_two_away, branch_two, down_x
+    )
+    down_sum = plus(rows_of(down_sum, line, 2), down_x)
+    down_z = trade(rows_of(down_sum, 1 - deep, 2), DEEP)
+    grad_mod_two = chunked(
+        mod_two + jnp.concatenate([arrived_a, arrived_b], axis=0).astype(F32)
+    )
+    grad_out = chunked(cot_low.astype(F32))
+    grad_halfway = grad_out + norm_back(
+        grad_mod_two * (1.0 + mods_own[4]), normed_two, inverse_two
+    )
+    grad_branch_one = flat((grad_halfway * mods_own[2]).astype(BF16))
+    grad_att_away = dot(proj_other, grad_branch_one, 1, 1).astype(BF16)
+    grad_att_away, grad_branch_one = fence(grad_att_away, grad_branch_one)
+
+    grad_att_other = swap(grad_att_away)
+    grad_att_own = dot(proj_weight, grad_branch_one, 1, 1).astype(BF16)
+    inputs_one = jnp.concatenate([inputs_one_own, inputs_one_other], axis=0)
+    grad_att_other, grad_att_own, down_z, branch_one_next, inputs_one = fence(
+        grad_att_other, grad_att_own, down_z, grad_branch_one, inputs_one
+    )
+    down_sum = plus(rows_of(down_sum, deep, 2), down_z)
+    down_far = trade(down_sum, FAR)
+
+    def back(out, lse, first):
+        return attend_back(
+            qkv_own,
+            qkv_other,
+            bias,
+            hot,
+            out,
+            grad_att_own.reshape(heads, HEAD_DIM, shard),
+            grad_att_other.reshape(heads, HEAD_DIM, shard),
+            lse,
+            first,
+            half_heads,
+        ).reshape(3 * half_width, pack)
+
+    def qkv_half(grad):
+        return lambda half: dot(rows_of(grad, half, 2), inputs_one, 1, 0)
+
+    grads_one_other = swap(branch_one_next)
+    grad_qkv_a = back(out_a, lse_a, 0)
+    grad_qkv_a, up_x = fence(grad_qkv_a, up_x)
+    up_sum = plus(rows_of(up_sum, line, 2), up_x)
+    up_z = trade(rows_of(up_sum, 1 - deep, 2), DEEP)
+    qkv_make = qkv_half(grad_qkv_a)
+    qkv_a_away = trade(qkv_make(1 - core).astype(BF16), CORE)
+    qkv_a = plus(qkv_make(core), qkv_a_away)
+    qkv_a, grad_att_own = fence(qkv_a, grad_att_own)
+    qkv_a_x = trade(rows_of(qkv_a, 1 - line, 2), LINE)
+    grad_qkv_b = back(out_b, lse_b, half_heads)
+    grad_qkv_b, qkv_a_x, up_z, down_far, grads_one_other = fence(
+        grad_qkv_b, qkv_a_x, up_z, down_far, grads_one_other
+    )
+    qkv_a = plus(rows_of(qkv_a, line, 2), qkv_a_x)
+    up_sum = plus(rows_of(up_sum, deep, 2), up_z)
+    up_far = trade(up_sum, FAR)
+    down_sum = plus(down_sum, down_far)
+    down_z = trade(down_sum, DEEP)
+    down_x = trade(down_sum, LINE)
+    weight_parts = weight_t.reshape(3, 2, half_width, width)
+    weight_a = weight_parts[:, 0].reshape(3 * half_width, width)
+    weight_b = weight_parts[:, 1].reshape(3 * half_width, width)
+    mod_one = dot(grad_qkv_a, weight_a, 0, 0) + dot(grad_qkv_b, weight_b, 0, 0)
+    mod_one_own, mod_one_away = chunked(mod_one[own_part]), chunked(mod_one[other_part])
+
+    def chunk_sums(own, other):
+        return jnp.concatenate([jnp.sum(own, axis=1), jnp.sum(other, axis=1)], axis=0)
+
+    gate_one_sums = jnp.sum(grad_halfway * chunked(branch_own), axis=1)
+    chunk_terms = jnp.concatenate(
+        [
+            chunk_sums(mod_one_own, mod_one_away),
+            chunk_sums(mod_one_own * normed_one, mod_one_away * normed_one_other),
+            jnp.concatenate([gate_one_sums, jnp.zeros_like(gate_one_sums)], axis=0),
+            chunk_sums(chunked(mod_two), chunked(mod_two_other)),
+            chunk_sums(
+                chunked(mod_two) * normed_two, chunked(mod_two_other) * normed_two_other
+            ),
+            chunk_sums(
+                chunked(branch_two) * grad_out,
+                chunked(branch_two_away) * chunked(cot_away.astype(F32)),
+            ),
+        ],
+        axis=1,
+    )
+    slot_terms = dot(chunk_hot, chunk_terms, 0, 0, HIGH).astype(BF16)
+    half = slot_terms.shape[1] // 2
+    low, high = slot_terms[:, :half], slot_terms[:, half:]
+    keep = jnp.where(position == 0, low, high)
+    away = jnp.where(position == 0, high, low)
+    qkv_make_b = qkv_half(grad_qkv_b)
+    qkv_b_away = trade(qkv_make_b(1 - core).astype(BF16), CORE)
+    qkv_b = plus(qkv_make_b(core), qkv_b_away)
+
+    def proj_half_of(half):
+        rows = rows_of(out_flat, half, 2)
+        return dot(rows[:, own_part], grad_branch_one, 1, 0) + dot(
+            rows[:, other_part], grads_one_other, 1, 0
+        )
+
+    proj_away = trade(proj_half_of(1 - core).astype(BF16), CORE)
+    proj_sum = plus(proj_half_of(core), proj_away)
+    away, keep, mod_one_next, qkv_b, proj_sum, down_z, down_x = fence(
+        away, keep, flat(mod_one_away).astype(BF16), qkv_b, proj_sum, down_z, down_x
+    )
+
+    grad_modulation = plus(keep, swap(away))[None]
+    mod_one_other = swap(mod_one_next)
+    gathered = jnp.concatenate([grad_modulation, trade(grad_modulation, CORE)], axis=0)
+    down_zx = trade(down_z, LINE)
+    proj_x = trade(rows_of(proj_sum, 1 - line, 2), LINE)
+    qkv_a_z = trade(rows_of(qkv_a, 1 - deep, 2), DEEP)
+    qkv_b_z = trade(rows_of(qkv_b, 1 - deep, 2), DEEP)
+    gathered, up_far, qkv_a_z, qkv_b_z, down_zx, proj_x = fence(
+        gathered, up_far, qkv_a_z, qkv_b_z, down_zx, proj_x
+    )
+    gathered = jnp.concatenate([gathered, trade(gathered, LINE)], axis=0)
+    up_sum = plus(up_sum, up_far)
+    up_x = trade(up_sum, LINE)
+    up_z = trade(up_sum, DEEP)
+    qkv_a = plus(rows_of(qkv_a, deep, 2), qkv_a_z)
+    qkv_a_far = trade(qkv_a, FAR)
+    qkv_b = plus(rows_of(qkv_b, deep, 2), qkv_b_z)
+    qkv_b_x = trade(rows_of(qkv_b, 1 - line, 2), LINE)
+    proj_sum = plus(rows_of(proj_sum, line, 2), proj_x)
+    gathered, up_x, up_z, qkv_a_far, qkv_b_x, mod_one_other, proj_sum = fence(
+        gathered, up_x, up_z, qkv_a_far, qkv_b_x, mod_one_other, proj_sum
+    )
+    gathered = jnp.concatenate(
+        [gathered, trade(gathered, DEEP), trade(gathered, FAR), trade(gathered, DEEP + FAR)], axis=0
+    )
+    up_zx = trade(up_z, LINE)
+    qkv_a = plus(qkv_a, qkv_a_far)
+    qkv_a_z = trade(qkv_a, DEEP)
+    qkv_b = plus(rows_of(qkv_b, line, 2), qkv_b_x)
+    qkv_b_far = trade(qkv_b, FAR)
+    proj_z = trade(rows_of(proj_sum, 1 - deep, 2), DEEP)
+    grad_mod_one = mod_one_own + chunked(mod_one_other.astype(F32))
+    grad_input = grad_halfway + norm_back(
+        grad_mod_one * (1.0 + mods_own[1]), normed_one, inverse_one
+    )
+    grad_input = flat(grad_input).astype(BF16)
+    gathered, up_zx, qkv_a_z, qkv_b_far, proj_z, grad_input, branch_two_next = fence(
+        gathered,
+        up_zx,
+        qkv_a_z,
+        qkv_b_far,
+        proj_z,
+        grad_input,
+        branch_two_away.astype(BF16),
+    )
+
+    def in_order(digit, own, other):
+        return jnp.where(
+            digit == 0,
+            jnp.concatenate([own, other], axis=0),
+            jnp.concatenate([other, own], axis=0),
+        ).reshape(3, HEAD_DIM, width)
+
+    qkv_a = in_order(deep, qkv_a, qkv_a_z)
+    qkv_a_x = trade(qkv_a, LINE)
+    qkv_b = plus(qkv_b, qkv_b_far)
+    qkv_b_x = trade(qkv_b, LINE)
+    proj_sum = plus(rows_of(proj_sum, deep, 2), proj_z)
+    proj_far = trade(proj_sum, FAR)
+    grad_mod_all = gathered.reshape(dp_size * slot_count, half)
+    grad_ada = dot(jax.nn.silu(condition_all).astype(BF16), grad_mod_all, 0, 0)
+    cond_part = dot(grad_mod_all, ada_weight, 1, 1).astype(BF16)
+    cond_part, qkv_b_x, proj_far, qkv_a_x, grad_ada = fence(
+        cond_part, qkv_b_x, proj_far, qkv_a_x, grad_ada
+    )
+    qkv_b = in_order(line, qkv_b, qkv_b_x)
+    qkv_b_z = trade(qkv_b, DEEP)
+    proj_sum = plus(proj_sum, proj_far)
+    proj_z = trade(proj_sum, DEEP)
+    grad_act = cond_part.astype(F32) + swap(cond_part).astype(F32)
+    grad_condition = jax.vjp(jax.nn.silu, condition_all)[1](grad_act)[0]
+    grad_class = dot(label_hot.astype(BF16), grad_condition.astype(BF16), 0, 0)
+    grad_time = dot(features_all, grad_condition, 0, 0, HIGH)
+    branch_two = chunked(branch_two) + chunked(swap(branch_two_next).astype(F32))
+    result = halfway + mods_own[5] * branch_two
+    proj_near = jnp.stack([proj_sum, proj_z])
+
+    def cores(near, far):
+        return [near, far, trade(near, CORE), trade(far, CORE)]
+
+    def digit(me, bits):
+        return me // bits % 2
+
+    def down_place(ref, me, group, block):
+        index = (
+            (digit(me, CORE) + group // 2) % 2 * 4
+            + (digit(me, LINE) + group % 2) % 2 * 2
+            + (digit(me, DEEP) + block) % 2
+        )
+        return ref.at[index]
+
+    def up_place(ref, me, group, block):
+        index = (digit(me, LINE) + group % 2) % 2 * 2 + (digit(me, DEEP) + block) % 2
+        column = (digit(me, CORE) + group // 2) % 2 * (hidden_width // 2)
+        return ref.at[index, :, pl.ds(pl.multiple_of(column, 128), hidden_width // 2)]
+
+    def qkv_place(offset, bits):
+        def place(ref, me, group, block):
+            unit = (
+                (digit(me, CORE) + group // 2) % 2 * 2 + (digit(me, bits) + group % 2) % 2
+            ) * 3 + block
+            return ref.at[unit // half_heads * heads + unit % half_heads + offset]
+
+        return place
+
+    grad_down = write_out(
+        cores(jnp.stack([down_sum, down_z]), jnp.stack([down_x, down_zx])),
+        down_place,
+        (8, hidden_width // 8, width),
+    )
+    grad_up = write_out(
+        cores(jnp.stack([up_sum, up_z]), jnp.stack([up_x, up_zx])),
+        up_place,
+        (4, width // 4, hidden_width),
+    )
+    grad_proj = write_out(
+        cores(proj_near, trade(proj_near, LINE)), down_place, (8, local_width // 8, width)
+    )
+    qkv_shape = (3 * heads, HEAD_DIM, width)
+    grad_qkv = write_out(cores(qkv_a, qkv_a_x), qkv_place(0, LINE), qkv_shape)
+    grad_qkv = write_out(cores(qkv_b, qkv_b_z), qkv_place(half_heads, DEEP), qkv_shape, grad_qkv)
+    return (
+        flat(result).astype(BF16)[None],
+        grad_input[None],
+        grad_class,
+        grad_time,
+        grad_ada,
+        grad_qkv.reshape(3, local_width, width).transpose(2, 0, 1),
+        grad_proj.reshape(local_width, width),
+        grad_up.reshape(width, hidden_width),
+        grad_down.reshape(hidden_width, width),
+    )
+
+
+def any_body(
     tokens,
     segments,
     labels,
@@ -256,8 +883,9 @@
 
 
 def solution(mesh):
+    pairs = mesh.shape["dp"] == 16 and mesh.shape["tensor"] == 2
     return jax.shard_map(
-        body,
+        pair_body if pairs else any_body,
         mesh=mesh,
         in_specs=(
             P("dp", "tensor", None),

time: 1220 us -> 496 us (0.41)
  waiting for transfers between devices: 766 us -> 119 us
  matrix products: 245 us -> 134 us
  Pallas kernels: 0 us -> 57.8 us
  starting transfers between devices: 9.72 us -> 64.5 us
  other arithmetic: 111 us -> 76.3 us
    psum x1 -> x0, waiting for transfers between devices: 468 us -> none  [body(): lax.psum(grad_class.astype(jnp.bfloat16), 'dp').astype(jnp.float32)]
    reduce_scatter x4 -> x0, waiting for transfers between devices: 146 us -> none  [the longest x1 60.1 us: body(): lax.psum_scatter(jnp.dot(attended, proj_weight, preferred_element_type=jn...]
    all_gather x4 -> x0, waiting for transfers between devices: 128 us -> none  [the longest x1 37.7 us: body(): inputs_one = lax.all_gather(modulated_one, 'tensor', axis=0, tiled=True)]
    ppermute x0 -> x70, waiting for transfers between devices: none -> 119 us  [the longest x53 76 us: trade(): return lax.ppermute(x, 'dp', [(i, i ^ bits) for i in range(dp_size)])]
    dot_general x35 -> x37, matrix products: 245 us -> 134 us  [dot(): lax.dot_general(left, right, (((left_dim,), (right_dim,)), ((), ())), pre...]
    ppermute x0 -> x70, starting transfers between devices: none -> 64.5 us  [the longest x53 46.8 us: trade(): return lax.ppermute(x, 'dp', [(i, i ^ bits) for i in range(dp_size)])]
    pallas_call x0 -> x9, Pallas kernels: none -> 57.8 us  [the longest x2 26.4 us: attend_back(): pl.pallas_call(functools.partial(attend_back_kernel, min(tokens, (1 << 19...]
    convert_element_type x14 -> x28, other arithmetic: 80.2 us -> 31.9 us  [the longest x15 9.74 us: plus(): return (a.astype(F32) + b.astype(F32)).astype(BF16)]
  transfers between devices with their start and end apart: 10 -> 70, of which waited for: 10 -> 26; matrix products, arithmetic and copies ran while one was open for 5% -> 38% of each run, Pallas kernels for 0% -> 11%
where the time goes in v2:
time: 496 us; the launch traced here: 487 us
  matrix products  134 us (27%)
  waiting for transfers between devices  119 us (24%)
  other arithmetic  76.3 us (15%)
  starting transfers between devices  64.5 us (13%)
  Pallas kernels  57.8 us (12%)
  local copies, waits for them, and re-layouts  31 us (6%)
    dot_general x37, matrix products, dot(): lax.dot_general(left, right, (((left_dim,), (right_dim,)), ((), ())), pre...  134 us
    ppermute x53, waiting for transfers between devices, trade(): return lax.ppermute(x, 'dp', [(i, i ^ bits) for i in range(dp_size)])  76 us
    ppermute x53, starting transfers between devices, trade(): return lax.ppermute(x, 'dp', [(i, i ^ bits) for i in range(dp_size)])  46.8 us
    ppermute x17, waiting for transfers between devices, swap(): return lax.ppermute(x, 'tensor', [(0, 1), (1, 0)])  43.4 us
    pallas_call x2, Pallas kernels, attend_back(): pl.pallas_call(functools.partial(attend_back_kernel, min(tokens, (1 << 19...  26.4 us
    ppermute x17, starting transfers between devices, swap(): return lax.ppermute(x, 'tensor', [(0, 1), (1, 0)])  17.7 us
    pallas_call x5, Pallas kernels, write_out(): pl.pallas_call(functools.partial(write_kernel, place, blocks, len(extra))...  15.9 us
    pallas_call x2, Pallas kernels, attend(): pl.pallas_call(functools.partial(attend_kernel, min(tokens, (1 << 20) //...  15.5 us
  transfers between devices with their start and end apart: 70, of which 26 were waited for; matrix products, arithmetic and copies ran while one was open for 38% of the time, Pallas kernels for 11%

profile of v2, /device:TPU:0, one launch (start us, length us, event | category | flops | bytes accessed | tf_op | source)
XLA Modules:
  0.0 486.5 jit_solution(5649224826842009686)
XLA Ops:
  2.5 3.0 collective-permute-start
  8.3 2.3 slice_bitcast_fusion
  10.7 3.9 fusion.94
  18.7 4.4 fusion.95
  23.1 7.2 %collective-permute-done.1 = bf16[192,1152]{1,0:T(8,128)(2,1)S(1)} collective-permute-done((bf16[192,1152]{1,0:T(8,128)(2,1)S(1)}, bf16[192,1152]{1,0:T(8,128)(2,1)S(1)}, u32[]{:S(2)}, u32[]{:S(2)}) %collective-permute-start.1) | collective-permute-done | bytes 442400 | tf_op jit(solution)/shard_map/ppermute | solution.py:259
  36.1 2.3 add_convert_fusion.4
  39.0 2.5 convolution_convert_fusion.4
  47.1 2.5 convolution_convert_fusion.3
  49.7 8.3 %shard_map.187 = (bf16[4,72,1024]{2,1,0:T(8,128)(2,1)}, f32[4,1,1024]{2,1,0:T(1,128)S(1)}) custom-call(bf16[24,72,512]{2,1,0:T(8,128)(2,1)S(1)} %bitcast.292, bf16[24,72,512]{2,1,0:T(8,128)(2,1)S(1)} %bitcast.304, bf16[24,72,512]{2,1,0:T(8,128)(2,1)S(1)} %bitcast.293, bf16[24,72,512]{2,1,0:T(8,128)(2,1)S(1)} %bitcast.305, ...), custom_call_target="tpu_custom_call" | custom-call | flops 1048576 | bytes 1048576 | tf_op jit(solution)/shard_map/pallas_call | solution.py:142
  60.0 7.1 %shard_map.188 = (bf16[4,72,1024]{2,1,0:T(8,128)(2,1)S(1)}, f32[4,1,1024]{2,1,0:T(1,128)S(1)}) custom-call(bf16[24,72,512]{2,1,0:T(8,128)(2,1)S(1)} %bitcast.295, bf16[24,72,512]{2,1,0:T(8,128)(2,1)S(1)} %bitcast.307, bf16[24,72,512]{2,1,0:T(8,128)(2,1)S(1)} %bitcast.296, bf16[24,72,512]{2,1,0:T(8,128)(2,1)S(1)} %bitcast.308, ...), custom_call_target="tpu_custom_call" | custom-call | flops 1048576 | bytes 1048576 | tf_op jit(solution)/shard_map/pallas_call | solution.py:142
  67.2 2.4 pad_maximum_fusion.8
  77.3 2.6 collective-permute-start.10
  79.9 3.0 collective-permute-start.11
  83.0 2.4 collective-permute-done.11
  88.6 5.0 %convolution_add_fusion.7 = f32[64,1152]{1,0:T(8,128)} fusion(f32[64,1152]{1,0:T(8,128)S(1)} %fusion.90, f32[1001,1152]{1,0:T(8,128)} %param.16, s32[64]{0:T(128)S(1)} %get-tuple-element.275), kind=kOutput, calls=%fused_computation.38 | convolution fusion | flops 885758528 | bytes 5202688 | tf_op jit(solution)/shard_map/dot_general | solution.py:21
  94.7 2.9 fusion.46
  100.3 2.7 add.378
  103.0 3.3 bitcast_add_fusion.3
  112.0 3.5 fusion.20
  116.0 2.4 multiply_reduce_fusion.3
  119.0 4.0 fusion.13
  125.6 11.6 %add_convert_fusion = (bf16[1024,2304]{1,0:T(8,128)(2,1)}, bf16[1024,2304]{1,0:T(8,128)(2,1)S(1)}) fusion(bf16[1024,1152]{1,0:T(8,128)(2,1)S(1)} %pad_maximum_fusion, bf16[1152,2304]{1,0:T(8,128)(2,1)S(1)} %bitcast.379), kind=kOutput, calls=%fused_computation.3 | convolution fusion | flops 5480644608 | bytes 17104896 | tf_op jit(solution)/shard_map/dot_general | solution.py:21
  138.2 4.8 convolution_convert_fusion.2
  143.1 10.8 %multiply_convert_fusion = bf16[1024,2304]{1,0:T(8,128)(2,1)S(1)} fusion(bf16[1024,2304]{1,0:T(8,128)(2,1)} %get-tuple-element.131, bf16[2304,1152]{1,0:T(8,128)(2,1)} %param.22, bf16[512,1152]{1,0:T(8,128)(2,1)} %copy-done.61, bf16[512,1152]{1,0:T(8,128)(2,1)} %copy-done.63), kind=kOutput, calls=%fused_computation.2 | convolution fusion | flops 5447614464 | bytes 17104896 | tf_op jit(solution)/shard_map/dot_general | solution.py:21
  154.0 8.3 %fusion = bf16[1152,1152]{1,0:T(8,128)(2,1)} fusion(bf16[1152,1152]{1,0:T(8,128)(2,1)} %collective-permute-done.15, bf16[1024,2304]{1,0:T(8,128)(2,1)S(1)} %copy-done.142, s32[]{:T(128)S(6)} %select_n.175, bf16[512,1152]{1,0:T(8,128)(2,1)S(1)} %copy-done.62, bf16[512,1152]{1,0:T(8,128)(2,1)S(1)} %copy-done.64), kind=kOutput, calls=%fused_computation.10 | convolution fusion | flops 2726608896 | bytes 10027012 | tf_op jit(solution)/shard_map/dot_general | solution.py:21
  162.3 7.7 %fusion.144 = (bf16[512,1152]{1,0:T(8,128)(2,1)}, f32[512,1152]{1,0:T(8,128)}) fusion(bf16[1152,2304]{1,0:T(8,128)(2,1)} %param.21, bf16[1024,2304]{1,0:T(8,128)(2,1)S(1)} %multiply_convert_fusion), kind=kOutput, calls=%fused_computation.314 | convolution fusion | flops 2718498816 | bytes 11206656 | tf_op jit(solution)/shard_map/dot_general | solution.py:21
  170.0 4.8 convolution_convert_fusion.1
  175.3 4.6 fusion.138
  183.2 6.1 %fusion.1 = bf16[1152,1152]{1,0:T(8,128)(2,1)S(1)} fusion(bf16[1024,1152]{1,0:T(8,128)(2,1)S(1)} %copy-done.45, bf16[1152,1152]{1,0:T(8,128)(2,1)} %collective-permute-done.17, bf16[1024,2304]{1,0:T(8,128)(2,1)S(1)} %copy-done.140, s32[]{:T(128)S(6)} %select_n.175), kind=kOutput, calls=%fused_computation.11 | convolution fusion | flops 2721890304 | bytes 10027012 | tf_op jit(solution)/shard_map/dot_general | solution.py:21
  189.3 6.0 %collective-permute-done.16 = bf16[256,1152]{1,0:T(8,128)(2,1)S(1)} collective-permute-done((bf16[256,1152]{1,0:T(8,128)(2,1)S(1)}, bf16[256,1152]{1,0:T(8,128)(2,1)S(1)}, u32[]{:S(2)}, u32[]{:S(2)}) %collective-permute-start.16) | collective-permute-done | bytes 589856 | tf_op jit(solution)/shard_map/ppermute | solution.py:259
  196.8 3.2 fusion.35
  202.7 5.1 %fusion.33 = f32[512,1152]{1,0:T(8,128)S(1)} fusion(bf16[2304,1152]{1,0:T(8,128)(2,1)S(1)} %bitcast.377, bf16[1024,2304]{1,0:T(8,128)(2,1)} %copy-done.141), kind=kOutput, calls=%fused_computation.93 | convolution fusion | flops 2717908992 | bytes 10027008 | tf_op jit(solution)/shard_map/dot_general | solution.py:21
  207.9 5.8 %fusion.37 = f32[512,1152]{1,0:T(8,128)S(1)} fusion(bf16[1152,2304]{1,0:T(8,128)(2,1)S(1)} %bitcast.381, bf16[1024,2304]{1,0:T(8,128)(2,1)} %copy-done.139), kind=kOutput, calls=%fused_computation.97 | convolution fusion | flops 2717908992 | bytes 10027008 | tf_op jit(solution)/shard_map/dot_general | solution.py:21
  213.8 2.8 fusion.45
  216.6 4.6 fusion.8
  226.3 2.6 fusion.74
  231.4 4.6 fusion.17
  236.4 4.2 collective-permute-done.21
  241.4 13.1 %shard_map.189 = bf16[3,4,72,1024]{3,2,1,0:T(8,128)(2,1)} custom-call(bf16[24,72,512]{2,1,0:T(8,128)(2,1)} %bitcast.298, bf16[24,72,512]{2,1,0:T(8,128)(2,1)} %bitcast.310, bf16[24,72,512]{2,1,0:T(8,128)(2,1)} %bitcast.299, bf16[24,72,512]{2,1,0:T(8,128)(2,1)} %bitcast.311, bf16[24,72,512]{2,1,0:T(8,128)(2,1)} %bitcast.300, bf16[24,72,512]{2,1,0:T(8,128)(2,1)} %bitcast.312, ...), custom_call_target="tpu_custom_call" | custom-call | flops 1048576 | bytes 1048576 | tf_op jit(solution)/shard_map/pallas_call | solution.py:163
  254.6 3.4 convolution_convert_fusion.6
  271.5 13.3 %shard_map.190 = bf16[3,4,72,1024]{3,2,1,0:T(8,128)(2,1)} custom-call(bf16[24,72,512]{2,1,0:T(8,128)(2,1)} %bitcast.301, bf16[24,72,512]{2,1,0:T(8,128)(2,1)} %bitcast.313, bf16[24,72,512]{2,1,0:T(8,128)(2,1)} %bitcast.302, bf16[24,72,512]{2,1,0:T(8,128)(2,1)} %bitcast.314, bf16[24,72,512]{2,1,0:T(8,128)(2,1)} %bitcast.303, bf16[24,72,512]{2,1,0:T(8,128)(2,1)} %bitcast.315, ...), custom_call_target="tpu_custom_call" | custom-call | flops 1048576 | bytes 1048576 | tf_op jit(solution)/shard_map/pallas_call | solution.py:163
  284.8 7.1 %collective-permute-done.26 = bf16[288,1152]{1,0:T(8,128)(2,1)} collective-permute-done((bf16[288,1152]{1,0:T(8,128)(2,1)}, bf16[288,1152]{1,0:T(8,128)(2,1)}, u32[]{:S(2)}, u32[]{:S(2)}) %collective-permute-start.26) | collective-permute-done | bytes 663584 | tf_op jit(solution)/shard_map/ppermute | solution.py:262
  291.9 3.7 collective-permute-done.25
  298.4 3.3 convolution_convert_fusion.5
  301.7 3.0 fusion.145
  304.7 3.1 convolution_add_fusion.2
  309.5 4.5 fusion.16
  318.3 2.7 collective-permute-start.34
  332.1 9.8 %collective-permute-done.35 = bf16[108,1152]{1,0:T(8,128)(2,1)S(1)} collective-permute-done((bf16[108,1152]{1,0:T(8,128)(2,1)S(1)}, bf16[108,1152]{1,0:T(8,128)(2,1)S(1)}, u32[]{:S(2)}, u32[]{:S(2)}) %collective-permute-start.35) | collective-permute-done | bytes 248864 | tf_op jit(solution)/shard_map/ppermute | solution.py:262
  342.6 8.0 %collective-permute-done.34 = bf16[288,1152]{1,0:T(8,128)(2,1)S(1)} collective-permute-done((bf16[288,1152]{1,0:T(8,128)(2,1)S(1)}, bf16[288,1152]{1,0:T(8,128)(2,1)S(1)}, u32[]{:S(2)}, u32[]{:S(2)}) %collective-permute-start.34) | collective-permute-done | bytes 663584 | tf_op jit(solution)/shard_map/ppermute | solution.py:262
  351.5 2.2 collective-permute-done.36
  359.0 12.0 %collective-permute-done.39 = bf16[2,4,3456]{2,1,0:T(4,128)(2,1)S(1)} collective-permute-done((bf16[2,4,3456]{2,1,0:T(4,128)(2,1)S(1)}, bf16[2,4,3456]{2,1,0:T(4,128)(2,1)S(1)}, u32[]{:S(2)}, u32[]{:S(2)}) %collective-permute-start.39) | collective-permute-done | bytes 55328 | tf_op jit(solution)/shard_map/ppermute | solution.py:262
  372.0 2.2 collective-permute-done.42
  374.3 3.0 collective-permute-done.43
  392.2 11.1 %collective-permute-done.51 = bf16[72,1152]{1,0:T(8,128)(2,1)S(1)} collective-permute-done((bf16[72,1152]{1,0:T(8,128)(2,1)S(1)}, bf16[72,1152]{1,0:T(8,128)(2,1)S(1)}, u32[]{:S(2)}, u32[]{:S(2)}) %collective-permute-start.51) | collective-permute-done | bytes 165920 | tf_op jit(solution)/shard_map/ppermute | solution.py:262
  412.8 8.2 %fusion.76 = f32[1152,3456]{1,0:T(8,128)} fusion(bf16[64,3456]{1,0:T(8,128)(2,1)S(1)} %reshape.576, f32[64,1152]{1,0:T(8,128)S(1)} %copy-done.38), kind=kOutput, calls=%fused_computation.185 | convolution fusion | flops 509976576 | bytes 16662528 | tf_op jit(solution)/shard_map/dot_general | solution.py:21
  421.0 2.6 convolution_convert_fusion.7
  430.9 24.4 %collective-permute-done.56 = bf16[64,1152]{1,0:T(8,128)(2,1)S(1)} collective-permute-done((bf16[64,1152]{1,0:T(8,128)(2,1)S(1)}, bf16[64,1152]{1,0:T(8,128)(2,1)S(1)}, u32[]{:S(2)}, u32[]{:S(2)}) %collective-permute-start.56) | collective-permute-done | bytes 147488 | tf_op jit(solution)/shard_map/ppermute | solution.py:259
  456.9 5.9 %shard_map.195 = f32[8,288,1152]{2,1,0:T(8,128)} custom-call(bf16[2,288,1152]{2,1,0:T(8,128)(2,1)S(1)} %pad_maximum_fusion.5.refs_0_, bf16[2,288,1152]{2,1,0:T(8,128)(2,1)S(1)} %pad_maximum_fusion.6.refs_1_, bf16[2,288,1152]{2,1,0:T(8,128)(2,1)} %collective-permute-done.68.refs_2_, bf16[2,288,1152]{2,1,0:T(8,128)(2,1)} %collective-permute-done.69.refs_3_), custom_call_target="tpu_custom_call" | custom-call | flops 1048576 | bytes 1048576 | tf_op jit(solution)/shard_map/pallas_call | solution.py:206
  462.8 3.0 collective-permute-done.63.refs_1_
  468.5 3.1 fusion.77
  471.6 2.2 shard_map.191.refs_4_
  475.1 3.3 fusion.11
  480.0 4.2 shard_map.194
  (550 shorter events, 145.7 us)
Async XLA Ops:
  2.5 15.4 %collective-permute-start = (bf16[128,1152]{1,0:T(8,128)(2,1)}, bf16[128,1152]{1,0:T(8,128)(2,1)S(1)}, u32[]{:S(2)}, u32[]{:S(2)}) collective-permute-start(bf16[128,1152]{1,0:T(8,128)(2,1)} %slice_bitcast_fusion.4), channel_id=1, source_target_pairs={{0,1},{1,0},{2,3},{3,2},{4,5},{5,4},{6,7},{7,6},{8,9},{9,8},{10,11... | collective-permute-start | bytes 884744 | tf_op jit(solution)/shard_map/ppermute | solution.py:259
  18.7 11.6 %collective-permute-start.1 = (bf16[192,1152]{1,0:T(8,128)(2,1)S(1)}, bf16[192,1152]{1,0:T(8,128)(2,1)S(1)}, u32[]{:S(2)}, u32[]{:S(2)}) collective-permute-start(bf16[192,1152]{1,0:T(8,128)(2,1)S(1)} %get-tuple-element.104), channel_id=1, source_target_pairs={{0,1},{1,0},{2,3},{3,2},{4,5},{5,4},{6,7},{7,6},{8,9},{9,8},{10,11... | collective-permute-start | bytes 1327112 | tf_op jit(solution)/shard_map/ppermute | solution.py:259
  30.3 4.8 collective-permute-start.2
  31.3 11.6 %collective-permute-start.3 = (bf16[192,1152]{1,0:T(8,128)(2,1)}, bf16[192,1152]{1,0:T(8,128)(2,1)S(1)}, u32[]{:S(2)}, u32[]{:S(2)}) collective-permute-start(bf16[192,1152]{1,0:T(8,128)(2,1)} %get-tuple-element.106), channel_id=1, source_target_pairs={{0,1},{1,0},{2,3},{3,2},{4,5},{5,4},{6,7},{7,6},{8,9},{9,8},{10,11... | collective-permute-start | bytes 1327112 | tf_op jit(solution)/shard_map/ppermute | solution.py:259
  44.9 22.2 %collective-permute-start.4 = (bf16[288,1152]{1,0:T(8,128)(2,1)S(1)}, bf16[288,1152]{1,0:T(8,128)(2,1)}, u32[]{:S(2)}, u32[]{:S(2)}) collective-permute-start(bf16[288,1152]{1,0:T(8,128)(2,1)S(1)} %copy-done.73), channel_id=1, source_target_pairs={{0,1},{1,0},{2,3},{3,2},{4,5},{5,4},{6,7},{7,6},{8,9},{9,8},{10,11... | collective-permute-start | bytes 1990664 | tf_op jit(solution)/shard_map/ppermute | solution.py:259
  58.6 28.9 %collective-permute-start.6 = (bf16[288,1024]{1,0:T(8,128)(2,1)}, bf16[288,1024]{1,0:T(8,128)(2,1)}, u32[]{:S(2)}, u32[]{:S(2)}) collective-permute-start(bf16[288,1024]{1,0:T(8,128)(2,1)} %bitcast.31), channel_id=1, source_target_pairs={{0,1},{1,0},{2,3},{3,2},{4,5},{5,4},{6,7},{7,6},{8,9},{9,8},{10,11... | collective-permute-start | bytes 1769480 | tf_op jit(solution)/shard_map/ppermute | solution.py:259
  69.6 28.1 %collective-permute-start.5 = (bf16[288,1024]{1,0:T(8,128)(2,1)S(1)}, bf16[288,1024]{1,0:T(8,128)(2,1)}, u32[]{:S(2)}, u32[]{:S(2)}) collective-permute-start(bf16[288,1024]{1,0:T(8,128)(2,1)S(1)} %bitcast.316), channel_id=1, source_target_pairs={{0,1},{1,0},{2,3},{3,2},{4,5},{5,4},{6,7},{7,6},{8,9},{9,8},{10,11... | collective-permute-start | bytes 1769480 | tf_op jit(solution)/shard_map/ppermute | solution.py:259
  70.9 14.5 %collective-permute-start.12 = (bf16[288,1152]{1,0:T(8,128)(2,1)}, bf16[288,1152]{1,0:T(8,128)(2,1)}, u32[]{:S(2)}, u32[]{:S(2)}) collective-permute-start(bf16[288,1152]{1,0:T(8,128)(2,1)} %collective-permute-done.4), channel_id=1, source_target_pairs={{0,2},{2,0},{4,6},{6,4},{8,10},{10,8},{12,14},{14,12},{16,18},{18,... | collective-permute-start | bytes 1990664 | tf_op jit(solution)/shard_map/ppermute | solution.py:262
  77.3 5.6 %collective-permute-start.10 = (s32[4,4,2]{1,2,0:T(2,128)S(1)}, s32[4,4,2]{1,2,0:T(2,128)S(1)}, u32[]{:S(2)}, u32[]{:S(2)}) collective-permute-start(s32[4,4,2]{1,2,0:T(2,128)S(1)} %pad_add_fusion), channel_id=1, source_target_pairs={{0,16},{2,18},{4,20},{6,22},{8,24},{10,26},{12,28},{14,30},{16,0},... | collective-permute-start | bytes 392 | tf_op jit(solution)/shard_map/ppermute | solution.py:262
  79.9 5.4 %collective-permute-start.11 = (s32[4,4,2]{1,2,0:T(2,128)S(1)}, s32[4,4,2]{1,2,0:T(2,128)S(1)}, u32[]{:S(2)}, u32[]{:S(2)}) collective-permute-start(s32[4,4,2]{1,2,0:T(2,128)S(1)} %pad_add_fusion), channel_id=1, source_target_pairs={{0,24},{2,26},{4,28},{6,30},{8,16},{10,18},{12,20},{14,22},{16,8},... | collective-permute-start | bytes 392 | tf_op jit(solution)/shard_map/ppermute | solution.py:262
  111.4 13.6 %collective-permute-start.13 = (bf16[256,1152]{1,0:T(8,128)(2,1)}, bf16[256,1152]{1,0:T(8,128)(2,1)S(1)}, u32[]{:S(2)}, u32[]{:S(2)}) collective-permute-start(bf16[256,1152]{1,0:T(8,128)(2,1)} %get-tuple-element.124), channel_id=1, source_target_pairs={{0,1},{1,0},{2,3},{3,2},{4,5},{5,4},{6,7},{7,6},{8,9},{9,8},{10,11... | collective-permute-start | bytes 1769480 | tf_op jit(solution)/shard_map/ppermute | solution.py:259
  125.0 12.2 %collective-permute-start.14 = (bf16[256,1152]{1,0:T(8,128)(2,1)S(1)}, bf16[256,1152]{1,0:T(8,128)(2,1)S(1)}, u32[]{:S(2)}, u32[]{:S(2)}) collective-permute-start(bf16[256,1152]{1,0:T(8,128)(2,1)S(1)} %copy-done.78), channel_id=1, source_target_pairs={{0,1},{1,0},{2,3},{3,2},{4,5},{5,4},{6,7},{7,6},{8,9},{9,8},{10,11... | collective-permute-start | bytes 1769480 | tf_op jit(solution)/shard_map/ppermute | solution.py:259
  143.0 11.0 %collective-permute-start.15 = (bf16[1152,1152]{1,0:T(8,128)(2,1)}, bf16[1152,1152]{1,0:T(8,128)(2,1)}, u32[]{:S(2)}, u32[]{:S(2)}) collective-permute-start(bf16[1152,1152]{1,0:T(8,128)(2,1)} %convolution_convert_fusion.2), channel_id=1, source_target_pairs={{0,2},{2,0},{4,6},{6,4},{8,10},{10,8},{12,14},{14,12},{16,18},{18,... | collective-permute-start | bytes 7962632 | tf_op jit(solution)/shard_map/ppermute | solution.py:262
  174.8 8.4 %collective-permute-start.17 = (bf16[1152,1152]{1,0:T(8,128)(2,1)}, bf16[1152,1152]{1,0:T(8,128)(2,1)}, u32[]{:S(2)}, u32[]{:S(2)}) collective-permute-start(bf16[1152,1152]{1,0:T(8,128)(2,1)} %convolution_convert_fusion.1), channel_id=1, source_target_pairs={{0,2},{2,0},{4,6},{6,4},{8,10},{10,8},{12,14},{14,12},{16,18},{18,... | collective-permute-start | bytes 7962632 | tf_op jit(solution)/shard_map/ppermute | solution.py:262
  180.0 15.4 %collective-permute-start.16 = (bf16[256,1152]{1,0:T(8,128)(2,1)S(1)}, bf16[256,1152]{1,0:T(8,128)(2,1)S(1)}, u32[]{:S(2)}, u32[]{:S(2)}) collective-permute-start(bf16[256,1152]{1,0:T(8,128)(2,1)S(1)} %get-tuple-element.230), channel_id=1, source_target_pairs={{0,1},{1,0},{2,3},{3,2},{4,5},{5,4},{6,7},{7,6},{8,9},{9,8},{10,11... | collective-permute-start | bytes 1769480 | tf_op jit(solution)/shard_map/ppermute | solution.py:259
  181.6 32.1 %collective-permute-start.19 = (bf16[576,1152]{1,0:T(8,128)(2,1)S(1)}, bf16[576,1152]{1,0:T(8,128)(2,1)S(1)}, u32[]{:S(2)}, u32[]{:S(2)}) collective-permute-start(bf16[576,1152]{1,0:T(8,128)(2,1)S(1)} %constant_dynamic-slice_fusion.9), channel_id=1, source_target_pairs={{0,4},{2,6},{4,0},{6,2},{8,12},{10,14},{12,8},{14,10},{16,20},{18,... | collective-permute-start | bytes 3981320 | tf_op jit(solution)/shard_map/ppermute | solution.py:262
  195.4 18.4 %collective-permute-start.18 = (bf16[256,1152]{1,0:T(8,128)(2,1)S(1)}, bf16[256,1152]{1,0:T(8,128)(2,1)S(1)}, u32[]{:S(2)}, u32[]{:S(2)}) collective-permute-start(bf16[256,1152]{1,0:T(8,128)(2,1)S(1)} %get-tuple-element.135), channel_id=1, source_target_pairs={{0,1},{1,0},{2,3},{3,2},{4,5},{5,4},{6,7},{7,6},{8,9},{9,8},{10,11... | collective-permute-start | bytes 1769480 | tf_op jit(solution)/shard_map/ppermute | solution.py:259
  201.3 53.3 %collective-permute-start.22 = (bf16[576,1152]{1,0:T(8,128)(2,1)}, bf16[576,1152]{1,0:T(8,128)(2,1)}, u32[]{:S(2)}, u32[]{:S(2)}) collective-permute-start(bf16[576,1152]{1,0:T(8,128)(2,1)} %constant_dynamic-slice_fusion.7), channel_id=1, source_target_pairs={{0,4},{2,6},{4,0},{6,2},{8,12},{10,14},{12,8},{14,10},{16,20},{18,... | collective-permute-start | bytes 3981320 | tf_op jit(solution)/shard_map/ppermute | solution.py:262
  222.1 14.2 %collective-permute-start.20 = (bf16[576,512]{1,0:T(8,128)(2,1)S(1)}, bf16[576,512]{1,0:T(8,128)(2,1)S(1)}, u32[]{:S(2)}, u32[]{:S(2)}) collective-permute-start(bf16[576,512]{1,0:T(8,128)(2,1)S(1)} %convolution_convert_fusion.9), channel_id=1, source_target_pairs={{0,1},{1,0},{2,3},{3,2},{4,5},{5,4},{6,7},{7,6},{8,9},{9,8},{10,11... | collective-permute-start | bytes 1769480 | tf_op jit(solution)/shard_map/ppermute | solution.py:259
  225.1 15.5 %collective-permute-start.21 = (bf16[288,1152]{1,0:T(8,128)(2,1)S(1)}, bf16[288,1152]{1,0:T(8,128)(2,1)S(1)}, u32[]{:S(2)}, u32[]{:S(2)}) collective-permute-start(bf16[288,1152]{1,0:T(8,128)(2,1)S(1)} %constant_dynamic-slice_fusion.8), channel_id=1, source_target_pairs={{0,8},{2,10},{4,12},{6,14},{8,0},{10,2},{12,4},{14,6},{16,24},{18,... | collective-permute-start | bytes 1990664 | tf_op jit(solution)/shard_map/ppermute | solution.py:262
  258.0 8.7 %collective-permute-start.23 = (bf16[432,1152]{1,0:T(8,128)(2,1)S(1)}, bf16[432,1152]{1,0:T(8,128)(2,1)S(1)}, u32[]{:S(2)}, u32[]{:S(2)}) collective-permute-start(bf16[432,1152]{1,0:T(8,128)(2,1)S(1)} %convolution_convert_fusion.6), channel_id=1, source_target_pairs={{0,2},{2,0},{4,6},{6,4},{8,10},{10,8},{12,14},{14,12},{16,18},{18,... | collective-permute-start | bytes 2985992 | tf_op jit(solution)/shard_map/ppermute | solution.py:262
  259.1 32.8 %collective-permute-start.26 = (bf16[288,1152]{1,0:T(8,128)(2,1)}, bf16[288,1152]{1,0:T(8,128)(2,1)}, u32[]{:S(2)}, u32[]{:S(2)}) collective-permute-start(bf16[288,1152]{1,0:T(8,128)(2,1)} %add_convert_fusion.8), channel_id=1, source_target_pairs={{0,16},{2,18},{4,20},{6,22},{8,24},{10,26},{12,28},{14,30},{16,0},... | collective-permute-start | bytes 1990664 | tf_op jit(solution)/shard_map/ppermute | solution.py:262
  260.9 34.7 %collective-permute-start.27 = (bf16[512,1152]{1,0:T(8,128)(2,1)S(1)}, bf16[512,1152]{1,0:T(8,128)(2,1)}, u32[]{:S(2)}, u32[]{:S(2)}) collective-permute-start(bf16[512,1152]{1,0:T(8,128)(2,1)S(1)} %get-tuple-element.157), channel_id=1, source_target_pairs={{0,1},{1,0},{2,3},{3,2},{4,5},{5,4},{6,7},{7,6},{8,9},{9,8},{10,11... | collective-permute-start | bytes 3538952 | tf_op jit(solution)/shard_map/ppermute | solution.py:259
  264.9 30.8 %collective-permute-start.25 = (bf16[288,1152]{1,0:T(8,128)(2,1)}, bf16[288,1152]{1,0:T(8,128)(2,1)}, u32[]{:S(2)}, u32[]{:S(2)}) collective-permute-start(bf16[288,1152]{1,0:T(8,128)(2,1)} %constant_dynamic-slice_fusion.5), channel_id=1, source_target_pairs={{0,8},{2,10},{4,12},{6,14},{8,0},{10,2},{12,4},{14,6},{16,24},{18,... | collective-permute-start | bytes 1990664 | tf_op jit(solution)/shard_map/ppermute | solution.py:262
  268.8 26.8 %collective-permute-start.24 = (bf16[216,1152]{1,0:T(8,128)(2,1)}, bf16[216,1152]{1,0:T(8,128)(2,1)}, u32[]{:S(2)}, u32[]{:S(2)}) collective-permute-start(bf16[216,1152]{1,0:T(8,128)(2,1)} %constant_dynamic-slice_fusion.6), channel_id=1, source_target_pairs={{0,4},{2,6},{4,0},{6,2},{8,12},{10,14},{12,8},{14,10},{16,20},{18,... | collective-permute-start | bytes 1493000 | tf_op jit(solution)/shard_map/ppermute | solution.py:262
  297.1 28.7 %collective-permute-start.30 = (bf16[288,1152]{1,0:T(8,128)(2,1)S(1)}, bf16[288,1152]{1,0:T(8,128)(2,1)S(1)}, u32[]{:S(2)}, u32[]{:S(2)}) collective-permute-start(bf16[288,1152]{1,0:T(8,128)(2,1)S(1)} %add_convert_fusion.7), channel_id=1, source_target_pairs={{0,8},{2,10},{4,12},{6,14},{8,0},{10,2},{12,4},{14,6},{16,24},{18,... | collective-permute-start | bytes 1990664 | tf_op jit(solution)/shard_map/ppermute | solution.py:262
  297.2 28.6 %collective-permute-start.31 = (bf16[288,1152]{1,0:T(8,128)(2,1)S(1)}, bf16[288,1152]{1,0:T(8,128)(2,1)S(1)}, u32[]{:S(2)}, u32[]{:S(2)}) collective-permute-start(bf16[288,1152]{1,0:T(8,128)(2,1)S(1)} %add_convert_fusion.7), channel_id=1, source_target_pairs={{0,4},{2,6},{4,0},{6,2},{8,12},{10,14},{12,8},{14,10},{16,20},{18,... | collective-permute-start | bytes 1990664 | tf_op jit(solution)/shard_map/ppermute | solution.py:262
  314.6 9.9 %collective-permute-start.28 = (bf16[432,1152]{1,0:T(8,128)(2,1)S(1)}, bf16[432,1152]{1,0:T(8,128)(2,1)S(1)}, u32[]{:S(2)}, u32[]{:S(2)}) collective-permute-start(bf16[432,1152]{1,0:T(8,128)(2,1)S(1)} %convolution_convert_fusion.5), channel_id=1, source_target_pairs={{0,2},{2,0},{4,6},{6,4},{8,10},{10,8},{12,14},{14,12},{16,18},{18,... | collective-permute-start | bytes 2985992 | tf_op jit(solution)/shard_map/ppermute | solution.py:262
  316.6 5.7 %collective-permute-start.29 = (bf16[288,1152]{1,0:T(8,128)(2,1)S(1)}, bf16[288,1152]{1,0:T(8,128)(2,1)S(1)}, u32[]{:S(2)}, u32[]{:S(2)}) collective-permute-start(bf16[288,1152]{1,0:T(8,128)(2,1)S(1)} %fusion.5), channel_id=1, source_target_pairs={{0,2},{2,0},{4,6},{6,4},{8,10},{10,8},{12,14},{14,12},{16,18},{18,... | collective-permute-start | bytes 1990664 | tf_op jit(solution)/shard_map/ppermute | solution.py:262
  318.3 32.3 %collective-permute-start.34 = (bf16[288,1152]{1,0:T(8,128)(2,1)S(1)}, bf16[288,1152]{1,0:T(8,128)(2,1)S(1)}, u32[]{:S(2)}, u32[]{:S(2)}) collective-permute-start(bf16[288,1152]{1,0:T(8,128)(2,1)S(1)} %add_convert_fusion.6), channel_id=1, source_target_pairs={{0,16},{2,18},{4,20},{6,22},{8,24},{10,26},{12,28},{14,30},{16,0},... | collective-permute-start | bytes 1990664 | tf_op jit(solution)/shard_map/ppermute | solution.py:262
  322.3 19.6 %collective-permute-start.35 = (bf16[108,1152]{1,0:T(8,128)(2,1)S(1)}, bf16[108,1152]{1,0:T(8,128)(2,1)S(1)}, u32[]{:S(2)}, u32[]{:S(2)}) collective-permute-start(bf16[108,1152]{1,0:T(8,128)(2,1)S(1)} %constant_dynamic-slice_fusion.4), channel_id=1, source_target_pairs={{0,8},{2,10},{4,12},{6,14},{8,0},{10,2},{12,4},{14,6},{16,24},{18,... | collective-permute-start | bytes 746504 | tf_op jit(solution)/shard_map/ppermute | solution.py:262
  326.7 27.0 %collective-permute-start.36 = (bf16[216,1152]{1,0:T(8,128)(2,1)S(1)}, bf16[216,1152]{1,0:T(8,128)(2,1)S(1)}, u32[]{:S(2)}, u32[]{:S(2)}) collective-permute-start(bf16[216,1152]{1,0:T(8,128)(2,1)S(1)} %constant_dynamic-slice_fusion.3), channel_id=1, source_target_pairs={{0,8},{2,10},{4,12},{6,14},{8,0},{10,2},{12,4},{14,6},{16,24},{18,... | collective-permute-start | bytes 1493000 | tf_op jit(solution)/shard_map/ppermute | solution.py:262
  328.5 25.2 %collective-permute-start.37 = (bf16[288,1152]{1,0:T(8,128)(2,1)S(1)}, bf16[288,1152]{1,0:T(8,128)(2,1)S(1)}, u32[]{:S(2)}, u32[]{:S(2)}) collective-permute-start(bf16[288,1152]{1,0:T(8,128)(2,1)S(1)} %collective-permute-done.30), channel_id=1, source_target_pairs={{0,4},{2,6},{4,0},{6,2},{8,12},{10,14},{12,8},{14,10},{16,20},{18,... | collective-permute-start | bytes 1990664 | tf_op jit(solution)/shard_map/ppermute | solution.py:262
  331.0 20.5 %collective-permute-start.38 = (bf16[144,1152]{1,0:T(8,128)(2,1)S(1)}, bf16[144,1152]{1,0:T(8,128)(2,1)S(1)}, u32[]{:S(2)}, u32[]{:S(2)}) collective-permute-start(bf16[144,1152]{1,0:T(8,128)(2,1)S(1)} %constant_dynamic-slice_fusion.2), channel_id=1, source_target_pairs={{0,4},{2,6},{4,0},{6,2},{8,12},{10,14},{12,8},{14,10},{16,20},{18,... | collective-permute-start | bytes 995336 | tf_op jit(solution)/shard_map/ppermute | solution.py:262
  341.8 35.5 %collective-permute-start.44 = (bf16[512,1152]{1,0:T(8,128)(2,1)S(1)}, bf16[512,1152]{1,0:T(8,128)(2,1)S(1)}, u32[]{:S(2)}, u32[]{:S(2)}) collective-permute-start(bf16[512,1152]{1,0:T(8,128)(2,1)S(1)} %slice.240), channel_id=1, source_target_pairs={{0,1},{1,0},{2,3},{3,2},{4,5},{5,4},{6,7},{7,6},{8,9},{9,8},{10,11... | collective-permute-start | bytes 3538952 | tf_op jit(solution)/shard_map/ppermute | solution.py:259
  353.9 23.4 %collective-permute-start.40 = (bf16[288,1152]{1,0:T(8,128)(2,1)S(1)}, bf16[288,1152]{1,0:T(8,128)(2,1)S(1)}, u32[]{:S(2)}, u32[]{:S(2)}) collective-permute-start(bf16[288,1152]{1,0:T(8,128)(2,1)S(1)} %add_convert_fusion.5), channel_id=1, source_target_pairs={{0,4},{2,6},{4,0},{6,2},{8,12},{10,14},{12,8},{14,10},{16,20},{18,... | collective-permute-start | bytes 1990664 | tf_op jit(solution)/shard_map/ppermute | solution.py:262
  354.9 22.4 %collective-permute-start.41 = (bf16[288,1152]{1,0:T(8,128)(2,1)S(1)}, bf16[288,1152]{1,0:T(8,128)(2,1)S(1)}, u32[]{:S(2)}, u32[]{:S(2)}) collective-permute-start(bf16[288,1152]{1,0:T(8,128)(2,1)S(1)} %add_convert_fusion.5), channel_id=1, source_target_pairs={{0,8},{2,10},{4,12},{6,14},{8,0},{10,2},{12,4},{14,6},{16,24},{18,... | collective-permute-start | bytes 1990664 | tf_op jit(solution)/shard_map/ppermute | solution.py:262
  355.4 15.6 %collective-permute-start.39 = (bf16[2,4,3456]{2,1,0:T(4,128)(2,1)S(1)}, bf16[2,4,3456]{2,1,0:T(4,128)(2,1)S(1)}, u32[]{:S(2)}, u32[]{:S(2)}) collective-permute-start(bf16[2,4,3456]{2,1,0:T(4,128)(2,1)S(1)} %pad_maximum_fusion.19), channel_id=1, source_target_pairs={{0,4},{2,6},{4,0},{6,2},{8,12},{10,14},{12,8},{14,10},{16,20},{18,... | collective-permute-start | bytes 165896 | tf_op jit(solution)/shard_map/ppermute | solution.py:262
  356.6 17.7 %collective-permute-start.42 = (bf16[108,1152]{1,0:T(8,128)(2,1)S(1)}, bf16[108,1152]{1,0:T(8,128)(2,1)S(1)}, u32[]{:S(2)}, u32[]{:S(2)}) collective-permute-start(bf16[108,1152]{1,0:T(8,128)(2,1)S(1)} %add_convert_fusion.15), channel_id=1, source_target_pairs={{0,16},{2,18},{4,20},{6,22},{8,24},{10,26},{12,28},{14,30},{16,0},... | collective-permute-start | bytes 746504 | tf_op jit(solution)/shard_map/ppermute | solution.py:262
  371.0 6.3 %collective-permute-start.43 = (bf16[108,1152]{1,0:T(8,128)(2,1)S(1)}, bf16[108,1152]{1,0:T(8,128)(2,1)S(1)}, u32[]{:S(2)}, u32[]{:S(2)}) collective-permute-start(bf16[108,1152]{1,0:T(8,128)(2,1)S(1)} %constant_dynamic-slice_fusion.1), channel_id=1, source_target_pairs={{0,4},{2,6},{4,0},{6,2},{8,12},{10,14},{12,8},{14,10},{16,20},{18,... | collective-permute-start | bytes 746504 | tf_op jit(solution)/shard_map/ppermute | solution.py:262
  374.3 53.2 %collective-permute-start.68 = (bf16[2,288,1152]{2,1,0:T(8,128)(2,1)S(1)}, bf16[2,288,1152]{2,1,0:T(8,128)(2,1)}, u32[]{:S(2)}, u32[]{:S(2)}) collective-permute-start(bf16[2,288,1152]{2,1,0:T(8,128)(2,1)S(1)} %pad_maximum_fusion.5.refs_0_), channel_id=1, source_target_pairs={{0,2},{2,0},{4,6},{6,4},{8,10},{10,8},{12,14},{14,12},{16,18},{18,... | collective-permute-start | bytes 3981320 | tf_op jit(solution)/shard_map/ppermute | solution.py:262
  377.4 10.6 %collective-permute-start.47 = (bf16[4,4,3456]{2,1,0:T(4,128)(2,1)S(1)}, bf16[4,4,3456]{2,1,0:T(4,128)(2,1)S(1)}, u32[]{:S(2)}, u32[]{:S(2)}) collective-permute-start(bf16[4,4,3456]{2,1,0:T(4,128)(2,1)S(1)} %pad_maximum_fusion.17), channel_id=1, source_target_pairs={{0,24},{2,26},{4,28},{6,30},{8,16},{10,18},{12,20},{14,22},{16,8},... | collective-permute-start | bytes 331784 | tf_op jit(solution)/shard_map/ppermute | solution.py:262
  379.2 9.7 %collective-permute-start.46 = (bf16[4,4,3456]{2,1,0:T(4,128)(2,1)S(1)}, bf16[4,4,3456]{2,1,0:T(4,128)(2,1)S(1)}, u32[]{:S(2)}, u32[]{:S(2)}) collective-permute-start(bf16[4,4,3456]{2,1,0:T(4,128)(2,1)S(1)} %pad_maximum_fusion.17), channel_id=1, source_target_pairs={{0,16},{2,18},{4,20},{6,22},{8,24},{10,26},{12,28},{14,30},{16,0},... | collective-permute-start | bytes 331784 | tf_op jit(solution)/shard_map/ppermute | solution.py:262
  379.9 10.5 %collective-permute-start.45 = (bf16[4,4,3456]{2,1,0:T(4,128)(2,1)S(1)}, bf16[4,4,3456]{2,1,0:T(4,128)(2,1)S(1)}, u32[]{:S(2)}, u32[]{:S(2)}) collective-permute-start(bf16[4,4,3456]{2,1,0:T(4,128)(2,1)S(1)} %pad_maximum_fusion.17), channel_id=1, source_target_pairs={{0,8},{2,10},{4,12},{6,14},{8,0},{10,2},{12,4},{14,6},{16,24},{18,... | collective-permute-start | bytes 331784 | tf_op jit(solution)/shard_map/ppermute | solution.py:262
  381.8 23.0 %collective-permute-start.48 = (bf16[288,1152]{1,0:T(8,128)(2,1)S(1)}, bf16[288,1152]{1,0:T(8,128)(2,1)}, u32[]{:S(2)}, u32[]{:S(2)}) collective-permute-start(bf16[288,1152]{1,0:T(8,128)(2,1)S(1)} %collective-permute-done.41), channel_id=1, source_target_pairs={{0,4},{2,6},{4,0},{6,2},{8,12},{10,14},{12,8},{14,10},{16,20},{18,... | collective-permute-start | bytes 1990664 | tf_op jit(solution)/shard_map/ppermute | solution.py:262
  388.0 15.3 %collective-permute-start.49 = (bf16[108,1152]{1,0:T(8,128)(2,1)S(1)}, bf16[108,1152]{1,0:T(8,128)(2,1)S(1)}, u32[]{:S(2)}, u32[]{:S(2)}) collective-permute-start(bf16[108,1152]{1,0:T(8,128)(2,1)S(1)} %add_convert_fusion.14), channel_id=1, source_target_pairs={{0,8},{2,10},{4,12},{6,14},{8,0},{10,2},{12,4},{14,6},{16,24},{18,... | collective-permute-start | bytes 746504 | tf_op jit(solution)/shard_map/ppermute | solution.py:262
  388.9 14.4 %collective-permute-start.50 = (bf16[108,1152]{1,0:T(8,128)(2,1)S(1)}, bf16[108,1152]{1,0:T(8,128)(2,1)S(1)}, u32[]{:S(2)}, u32[]{:S(2)}) collective-permute-start(bf16[108,1152]{1,0:T(8,128)(2,1)S(1)} %add_convert_fusion.13), channel_id=1, source_target_pairs={{0,16},{2,18},{4,20},{6,22},{8,24},{10,26},{12,28},{14,30},{16,0},... | collective-permute-start | bytes 746504 | tf_op jit(solution)/shard_map/ppermute | solution.py:262
  390.4 12.9 %collective-permute-start.51 = (bf16[72,1152]{1,0:T(8,128)(2,1)S(1)}, bf16[72,1152]{1,0:T(8,128)(2,1)S(1)}, u32[]{:S(2)}, u32[]{:S(2)}) collective-permute-start(bf16[72,1152]{1,0:T(8,128)(2,1)S(1)} %constant_dynamic-slice_fusion), channel_id=1, source_target_pairs={{0,8},{2,10},{4,12},{6,14},{8,0},{10,2},{12,4},{14,6},{16,24},{18,... | collective-permute-start | bytes 497672 | tf_op jit(solution)/shard_map/ppermute | solution.py:262
  403.3 24.7 %collective-permute-start.69 = (bf16[2,288,1152]{2,1,0:T(8,128)(2,1)S(1)}, bf16[2,288,1152]{2,1,0:T(8,128)(2,1)}, u32[]{:S(2)}, u32[]{:S(2)}) collective-permute-start(bf16[2,288,1152]{2,1,0:T(8,128)(2,1)S(1)} %pad_maximum_fusion.6.refs_1_), channel_id=1, source_target_pairs={{0,2},{2,0},{4,6},{6,4},{8,10},{10,8},{12,14},{14,12},{16,18},{18,... | collective-permute-start | bytes 3981320 | tf_op jit(solution)/shard_map/ppermute | solution.py:262
  407.1 16.7 %collective-permute-start.53 = (bf16[108,1152]{1,0:T(8,128)(2,1)S(1)}, bf16[108,1152]{1,0:T(8,128)(2,1)S(1)}, u32[]{:S(2)}, u32[]{:S(2)}) collective-permute-start(bf16[108,1152]{1,0:T(8,128)(2,1)S(1)} %add_convert_fusion.12), channel_id=1, source_target_pairs={{0,4},{2,6},{4,0},{6,2},{8,12},{10,14},{12,8},{14,10},{16,20},{18,... | collective-permute-start | bytes 746504 | tf_op jit(solution)/shard_map/ppermute | solution.py:262
  409.3 14.4 %collective-permute-start.54 = (bf16[72,1152]{1,0:T(8,128)(2,1)S(1)}, bf16[72,1152]{1,0:T(8,128)(2,1)S(1)}, u32[]{:S(2)}, u32[]{:S(2)}) collective-permute-start(bf16[72,1152]{1,0:T(8,128)(2,1)S(1)} %add_convert_fusion.17), channel_id=1, source_target_pairs={{0,16},{2,18},{4,20},{6,22},{8,24},{10,26},{12,28},{14,30},{16,0},... | collective-permute-start | bytes 497672 | tf_op jit(solution)/shard_map/ppermute | solution.py:262
  411.6 14.7 %collective-permute-start.55 = (bf16[3,72,1152]{2,1,0:T(8,128)(2,1)S(1)}, bf16[3,72,1152]{2,1,0:T(8,128)(2,1)S(1)}, u32[]{:S(2)}, u32[]{:S(2)}) collective-permute-start(bf16[3,72,1152]{2,1,0:T(8,128)(2,1)S(1)} %bitcast.320), channel_id=1, source_target_pairs={{0,4},{2,6},{4,0},{6,2},{8,12},{10,14},{12,8},{14,10},{16,20},{18,... | collective-permute-start | bytes 1493000 | tf_op jit(solution)/shard_map/ppermute | solution.py:262
  423.8 44.7 %collective-permute-start.52 = (bf16[512,1152]{1,0:T(8,128)(2,1)S(1)}, bf16[512,1152]{1,0:T(8,128)(2,1)S(1)}, u32[]{:S(2)}, u32[]{:S(2)}) collective-permute-start(bf16[512,1152]{1,0:T(8,128)(2,1)S(1)} %copy-done.59), channel_id=1, source_target_pairs={{0,1},{1,0},{2,3},{3,2},{4,5},{5,4},{6,7},{7,6},{8,9},{9,8},{10,11... | collective-permute-start | bytes 3538952 | tf_op jit(solution)/shard_map/ppermute | solution.py:259
  426.3 29.0 %collective-permute-start.56 = (bf16[64,1152]{1,0:T(8,128)(2,1)S(1)}, bf16[64,1152]{1,0:T(8,128)(2,1)S(1)}, u32[]{:S(2)}, u32[]{:S(2)}) collective-permute-start(bf16[64,1152]{1,0:T(8,128)(2,1)S(1)} %convolution_convert_fusion.7), channel_id=1, source_target_pairs={{0,1},{1,0},{2,3},{3,2},{4,5},{5,4},{6,7},{7,6},{8,9},{9,8},{10,11... | collective-permute-start | bytes 442376 | tf_op jit(solution)/shard_map/ppermute | solution.py:259
  427.5 28.4 %collective-permute-start.57 = (bf16[3,72,1152]{2,1,0:T(8,128)(2,1)S(1)}, bf16[3,72,1152]{2,1,0:T(8,128)(2,1)S(1)}, u32[]{:S(2)}, u32[]{:S(2)}) collective-permute-start(bf16[3,72,1152]{2,1,0:T(8,128)(2,1)S(1)} %bitcast.317), channel_id=1, source_target_pairs={{0,8},{2,10},{4,12},{6,14},{8,0},{10,2},{12,4},{14,6},{16,24},{18,... | collective-permute-start | bytes 1493000 | tf_op jit(solution)/shard_map/ppermute | solution.py:262
  428.0 28.9 %collective-permute-start.61 = (bf16[3,72,1152]{2,1,0:T(8,128)(2,1)S(1)}, bf16[3,72,1152]{2,1,0:T(8,128)(2,1)S(1)}, u32[]{:S(2)}, u32[]{:S(2)}) collective-permute-start(bf16[3,72,1152]{2,1,0:T(8,128)(2,1)S(1)} %collective-permute-done.55.refs_1_), channel_id=1, source_target_pairs={{0,2},{2,0},{4,6},{6,4},{8,10},{10,8},{12,14},{14,12},{16,18},{18,... | collective-permute-start | bytes 1493000 | tf_op jit(solution)/shard_map/ppermute | solution.py:262
  428.0 27.4 %collective-permute-start.62 = (bf16[72,1152]{1,0:T(8,128)(2,1)S(1)}, bf16[72,1152]{1,0:T(8,128)(2,1)S(1)}, u32[]{:S(2)}, u32[]{:S(2)}) collective-permute-start(bf16[72,1152]{1,0:T(8,128)(2,1)S(1)} %add_convert_fusion.16), channel_id=1, source_target_pairs={{0,8},{2,10},{4,12},{6,14},{8,0},{10,2},{12,4},{14,6},{16,24},{18,... | collective-permute-start | bytes 497672 | tf_op jit(solution)/shard_map/ppermute | solution.py:262
  455.3 24.7 %collective-permute-start.66 = (bf16[2,288,1152]{2,1,0:T(8,128)(2,1)S(1)}, bf16[2,288,1152]{2,1,0:T(8,128)(2,1)S(1)}, u32[]{:S(2)}, u32[]{:S(2)}) collective-permute-start(bf16[2,288,1152]{2,1,0:T(8,128)(2,1)S(1)} %copy-done.4), channel_id=1, source_target_pairs={{0,2},{2,0},{4,6},{6,4},{8,10},{10,8},{12,14},{14,12},{16,18},{18,... | collective-permute-start | bytes 3981320 | tf_op jit(solution)/shard_map/ppermute | solution.py:262
  455.3 24.7 %collective-permute-start.67 = (bf16[2,288,1152]{2,1,0:T(8,128)(2,1)S(1)}, bf16[2,288,1152]{2,1,0:T(8,128)(2,1)S(1)}, u32[]{:S(2)}, u32[]{:S(2)}) collective-permute-start(bf16[2,288,1152]{2,1,0:T(8,128)(2,1)S(1)} %pad_maximum_fusion.4.refs_1_), channel_id=1, source_target_pairs={{0,2},{2,0},{4,6},{6,4},{8,10},{10,8},{12,14},{14,12},{16,18},{18,... | collective-permute-start | bytes 3981320 | tf_op jit(solution)/shard_map/ppermute | solution.py:262
  455.9 9.8 %collective-permute-start.63 = (bf16[2,72,1152]{2,1,0:T(8,128)(2,1)S(1)}, bf16[2,72,1152]{2,1,0:T(8,128)(2,1)S(1)}, u32[]{:S(2)}, u32[]{:S(2)}) collective-permute-start(bf16[2,72,1152]{2,1,0:T(8,128)(2,1)S(1)} %pad_maximum_fusion.16.refs_0_), channel_id=1, source_target_pairs={{0,4},{2,6},{4,0},{6,2},{8,12},{10,14},{12,8},{14,10},{16,20},{18,... | collective-permute-start | bytes 995336 | tf_op jit(solution)/shard_map/ppermute | solution.py:262
  456.9 8.9 %collective-permute-start.64 = (bf16[2,72,1152]{2,1,0:T(8,128)(2,1)S(1)}, bf16[2,72,1152]{2,1,0:T(8,128)(2,1)S(1)}, u32[]{:S(2)}, u32[]{:S(2)}) collective-permute-start(bf16[2,72,1152]{2,1,0:T(8,128)(2,1)S(1)} %pad_maximum_fusion.16.refs_0_), channel_id=1, source_target_pairs={{0,2},{2,0},{4,6},{6,4},{8,10},{10,8},{12,14},{14,12},{16,18},{18,... | collective-permute-start | bytes 995336 | tf_op jit(solution)/shard_map/ppermute | solution.py:262
  465.8 18.4 %collective-permute-start.58 = (bf16[3,72,1152]{2,1,0:T(8,128)(2,1)S(1)}, bf16[3,72,1152]{2,1,0:T(8,128)(2,1)S(1)}, u32[]{:S(2)}, u32[]{:S(2)}) collective-permute-start(bf16[3,72,1152]{2,1,0:T(8,128)(2,1)S(1)} %bitcast.318), channel_id=1, source_target_pairs={{0,2},{2,0},{4,6},{6,4},{8,10},{10,8},{12,14},{14,12},{16,18},{18,... | collective-permute-start | bytes 1493000 | tf_op jit(solution)/shard_map/ppermute | solution.py:262
  465.8 18.4 %collective-permute-start.59 = (bf16[3,72,1152]{2,1,0:T(8,128)(2,1)S(1)}, bf16[3,72,1152]{2,1,0:T(8,128)(2,1)S(1)}, u32[]{:S(2)}, u32[]{:S(2)}) collective-permute-start(bf16[3,72,1152]{2,1,0:T(8,128)(2,1)S(1)} %collective-permute-done.57.refs_1_), channel_id=1, source_target_pairs={{0,2},{2,0},{4,6},{6,4},{8,10},{10,8},{12,14},{14,12},{16,18},{18,... | collective-permute-start | bytes 1493000 | tf_op jit(solution)/shard_map/ppermute | solution.py:262
  468.5 9.9 %collective-permute-start.65 = (bf16[2,72,1152]{2,1,0:T(8,128)(2,1)S(1)}, bf16[2,72,1152]{2,1,0:T(8,128)(2,1)S(1)}, u32[]{:S(2)}, u32[]{:S(2)}) collective-permute-start(bf16[2,72,1152]{2,1,0:T(8,128)(2,1)S(1)} %collective-permute-done.63.refs_1_), channel_id=1, source_target_pairs={{0,2},{2,0},{4,6},{6,4},{8,10},{10,8},{12,14},{14,12},{16,18},{18,... | collective-permute-start | bytes 995336 | tf_op jit(solution)/shard_map/ppermute | solution.py:262
  (159 other events, 1177.9 us)
